TPU v7x, 256 devices: a whole 4x4x8 slice. The times are simulated.
256 devices in a mesh: row: 8 (over z), col: 32 (over x, y, core).
Axes of the slice: x: 4, y: 4, z: 8, core: 2. Of those that a mesh axis runs over, the one named last changes fastest.
Arguments:
- source_points: bfloat16 [64, 32768], P('col', 'row'), may hold values from -1 to 1
- target_points: bfloat16 [64, 131072], P('row', 'col'), may hold values from -0.8984375 to 0.8984375
- target_potential: float32 [131072], P('col'), may hold values from -2 to 8
Outputs:
- source_new: float32 [32768], P('row')
- target_new: float32 [131072], P('col')
All inputs are finite; a program needn't handle non-finite values.
Results may differ from a plain program's by a relative error of at most 0.0003.
Values may be sent and summed in bfloat16 or wider, within the bound.
No kernel may reach another device: no remote copies, remote signals or barrier semaphores. Data moves between devices by JAX's collectives and lax.ppermute only.
A program may use at most 64 MiB of HBM per device.

v0:
```python
import functools
import math

import jax
import jax.numpy as jnp
from jax import lax
from jax.experimental import pallas as pl
from jax.experimental.pallas import tpu as pltpu
from jax.sharding import PartitionSpec as P

EPS = 0.05
LN2 = math.log(2.0)
KAPPA = 1.0 / (EPS * LN2)
ROWS = 128
LANES = 1024
EXACT_LANES = 256
KEPT = 8
HEAD = 40.0


def split3(v):
    hi = v.astype(jnp.bfloat16)
    rest = v - hi.astype(jnp.float32)
    mid = rest.astype(jnp.bfloat16)
    low = (rest - mid.astype(jnp.float32)).astype(jnp.bfloat16)
    return hi, mid, low


def fill_operands(streamed, fixed, bias, lhs, rhs):
    d, n = streamed.shape
    hi, mid, low = split3(bias)
    row = lax.broadcasted_iota(jnp.int32, (d, n), 0)
    rows = jnp.where(row == 0, hi.astype(jnp.float32), 0.0)
    rows = jnp.where(row == 1, mid.astype(jnp.float32), rows)
    rows = jnp.where(row == 2, low.astype(jnp.float32), rows)
    points = streamed.astype(jnp.float32)
    lhs[:, : 2 * d] = jnp.concatenate([points, rows], axis=0).T.astype(jnp.bfloat16)
    lhs[:, 2 * d :] = jnp.concatenate([points, points], axis=0).T.astype(jnp.bfloat16)
    hi, mid, low = split3(fixed.astype(jnp.float32) * (2.0 * KAPPA))
    rhs[:d] = hi
    rhs[d : 2 * d] = jnp.where(row < 3, 1.0, 0.0).astype(jnp.bfloat16)
    rhs[2 * d : 3 * d] = mid
    rhs[3 * d :] = low


def scores_of(lhs, start, weights):
    scores = jnp.dot(lhs[pl.ds(start, ROWS), :], weights, preferred_element_type=jnp.float32)
    return scores.reshape(ROWS // 8, 8, weights.shape[1])


def lanes_of(step, width):
    return pl.ds(pl.multiple_of(step * width, width), width)


def exact_lse(lhs, rhs, out, offset):
    def block(step, carry):
        lanes = lanes_of(step, EXACT_LANES)
        weights = rhs[:, lanes]

        def rows(k, state):
            peak, total = state
            scores = scores_of(lhs, pl.multiple_of(k * ROWS, ROWS), weights)
            new_peak = jnp.maximum(peak, scores.max(0))
            total = total * jnp.exp2(peak - new_peak) + jnp.exp2(scores - new_peak[None]).sum(0)
            return new_peak, total

        start = (jnp.full((8, EXACT_LANES), -jnp.inf, jnp.float32), jnp.zeros((8, EXACT_LANES), jnp.float32))
        peak, total = lax.fori_loop(0, lhs.shape[0] // ROWS, rows, start)
        top = peak.max(0, keepdims=True)
        lse = offset + top + jnp.log2((total * jnp.exp2(peak - top)).sum(0, keepdims=True))
        out[:, lanes] = jnp.broadcast_to(lse, (out.shape[0], EXACT_LANES))
        return carry

    lax.fori_loop(0, rhs.shape[1] // EXACT_LANES, block, 0)


def in_range(sums):
    return jnp.logical_and(jnp.min(sums) > 2.0**-90, jnp.max(sums) < 2.0**127)


def square_norm(points):
    return jnp.sum(jnp.square(points.astype(jnp.float32)), axis=0, keepdims=True)


def lse_of(parts):
    top = parts.max(0, keepdims=True)
    return top + jnp.log2(jnp.exp2(parts - top).sum(0, keepdims=True))


def joined(pieces):
    return jnp.concatenate([piece[...].astype(jnp.float32) for piece in pieces], axis=0)


def first_kernel(order, pot, src_near, src_far, *refs):
    tgt_pieces, weights, (out, shift, flag, src, tgt, lhs, rhs) = refs[: -7 - KEPT], refs[-7 - KEPT : -7], refs[-7:]
    share = weights[0].shape[0]
    tgt[...] = joined(tgt_pieces).astype(jnp.bfloat16)
    features = joined([src_near, src_far]).astype(jnp.bfloat16)
    src[...] = jnp.dot(order[...], features, preferred_element_type=jnp.float32).astype(jnp.bfloat16)
    bias = KAPPA * (pot[...] - square_norm(tgt[...]))
    offset = jnp.max(bias, axis=1, keepdims=True) - HEAD
    shift[...] = bias - offset
    fill_operands(tgt[...], src[...], bias - offset, lhs, rhs)

    def block(step, carry):
        lanes = lanes_of(step, LANES)
        fixed = rhs[:, lanes]
        total = jnp.zeros((8, LANES), jnp.float32)
        for start in range(0, lhs.shape[0], ROWS):
            powers = jnp.exp2(scores_of(lhs, start, fixed))
            total = total + powers.sum(0)
            at = start % share
            weights[start // share][at : at + ROWS, lanes] = powers.reshape(ROWS, LANES).astype(jnp.bfloat16)
        out[:, lanes] = total.sum(0, keepdims=True)
        return carry

    lax.fori_loop(0, rhs.shape[1] // LANES, block, 0)
    sums = out[...]
    good = in_range(sums)
    flag[0, 0] = good.astype(jnp.int32)
    out[...] = offset + jnp.log2(sums)

    @pl.when(jnp.logical_not(good))
    def _():
        exact_lse(lhs, rhs, out, offset)


def second_kernel(tgt_total, src_total, lse, flag, shift, src, tgt, *refs):
    weights, (new, base, out, factors, lhs, rhs) = refs[:KEPT], refs[KEPT:]
    share, n_src = weights[0].shape
    bias = math.log2(tgt_total) - lse[...]
    new[...] = square_norm(src[...]) + EPS * LN2 * bias
    base[...] = square_norm(tgt[...]) + EPS * math.log(src_total)
    top = jnp.max(bias, axis=1, keepdims=True)
    factors[...] = jnp.broadcast_to(jnp.exp2(bias - top), (8, n_src))

    for part in range(KEPT):

        def block(step, carry):
            rows = lanes_of(step, 128)
            total = jnp.zeros((16, 8, 128), jnp.float32)
            for start in range(0, n_src, 128):
                powers = weights[part][rows, start : start + 128].astype(jnp.float32).reshape(16, 8, 128)
                total = total + powers * factors[:, start : start + 128][None]
            sums = total.reshape(128, 128).T.sum(0, keepdims=True)
            out[:, lanes_of(step + part * (share // 128), 128)] = jnp.broadcast_to(sums, (out.shape[0], 128))
            return carry

        lax.fori_loop(0, share // 128, block, 0)
    sums = out[...]
    good = jnp.logical_and(in_range(sums), jnp.min(bias) - jnp.max(bias) > -120.0)
    good = jnp.logical_and(good, flag[0, 0] == 1)
    out[...] = top - shift[...] + jnp.log2(sums)

    @pl.when(jnp.logical_not(good))
    def _():
        fill_operands(src[...], tgt[...], bias, lhs, rhs)
        exact_lse(lhs, rhs, out, 0.0)


ROW, X, Y, CORE = 8, 4, 4, 2


def from_row(v, k):
    return lax.ppermute(v, "row", [((z + k) % ROW, z) for z in range(ROW)])


def from_col(v, kx, ky, kc):
    pairs = []
    for x in range(X):
        for y in range(Y):
            for c in range(CORE):
                there = (((x + kx) % X) * Y + (y + ky) % Y) * CORE + (c + kc) % CORE
                pairs.append((there, (x * Y + y) * CORE + c))
    return lax.ppermute(v, "col", pairs)


def pair_lse(a, b):
    top = jnp.maximum(a, b)
    return top + jnp.log2(jnp.exp2(a - top) + jnp.exp2(b - top))


def ring_lse(own, others):
    top = jnp.maximum(jnp.maximum(own, others[1]), jnp.maximum(others[0], others[2]))
    near = jnp.exp2(others[0] - top) + jnp.exp2(others[2] - top)
    return top + jnp.log2((jnp.exp2(own - top) + jnp.exp2(others[1] - top)) + near)


def all_to_all(parts, axis):
    return lax.all_to_all(parts, axis, 0, 0, tiled=True)


def feature_order(per_src, per_tgt):
    col, row = lax.axis_index("col"), lax.axis_index("row")
    depth = per_src * X * Y * CORE
    at = lax.broadcasted_iota(jnp.int32, (depth, depth), 1)
    kx, ky, kc = (at // per_src) % X, (at // (per_src * X)) % Y, at // (per_src * X * Y)
    x, y, c = col // (Y * CORE), (col // CORE) % Y, col % CORE
    there = (((x + kx) % X) * Y + (y + ky) % Y) * CORE + (c + kc) % CORE
    src_feature = there * per_src + at % per_src
    at = lax.broadcasted_iota(jnp.int32, (depth, depth), 0)
    tgt_feature = ((row + at // per_tgt) % ROW) * per_tgt + at % per_tgt
    return (src_feature == tgt_feature).astype(jnp.bfloat16)


def on_device(source_points, target_points, target_potential):
    per_src, n_src = source_points.shape
    per_tgt, n_tgt = target_points.shape
    tgt_total = n_tgt * X * Y * CORE
    src_total = n_src * ROW
    dim = per_src * X * Y * CORE
    order = feature_order(per_src, per_tgt)

    up = [target_points]
    down = [target_points]
    src = source_points
    src = jnp.concatenate([src] + [from_col(src, k, 0, 0) for k in range(1, X)], axis=0)
    for _ in range(ROW // 2 - 1):
        up.append(from_row(up[-1], 1))
        down.append(from_row(down[-1], -1))
    down.append(from_row(down[-1], -1))
    src = jnp.concatenate([src] + [from_col(src, 0, k, 0) for k in range(1, Y)], axis=0)
    far = from_col(src, 0, 0, 1)
    tgt_pieces = up + down[:0:-1]

    params = pltpu.CompilerParams(vmem_limit_bytes=16 * 2**20)
    f32, bf16 = jnp.float32, jnp.bfloat16
    whole, scalar = pl.BlockSpec(memory_space=pltpu.VMEM), pl.BlockSpec(memory_space=pltpu.SMEM)
    *weights, lse, shift, flag, src, tgt = pl.pallas_call(
        first_kernel,
        out_shape=[
            *[pltpu.VMEM((n_tgt // KEPT, n_src), bf16)] * KEPT,
            jax.ShapeDtypeStruct((1, n_src), f32),
            jax.ShapeDtypeStruct((1, n_tgt), f32),
            jax.ShapeDtypeStruct((1, 1), jnp.int32),
            jax.ShapeDtypeStruct((dim, n_src), bf16),
            jax.ShapeDtypeStruct((dim, n_tgt), bf16),
        ],
        out_specs=[whole] * KEPT + [whole, whole, scalar, whole, whole],
        scratch_shapes=[pltpu.VMEM((n_tgt, 4 * dim), bf16), pltpu.VMEM((4 * dim, n_src), bf16)],
        compiler_params=params,
        name="first_pass",
    )(order, target_potential.reshape(1, n_tgt), src, far, *tgt_pieces)

    lse = lse.reshape(n_src)
    lse = pair_lse(lse, from_col(lse, 0, 0, 1))
    lse = ring_lse(lse, [from_col(lse, k, 0, 0) for k in (1, 2, 3)])
    lse = ring_lse(lse, [from_col(lse, 0, k, 0) for k in (1, 2, 3)])

    source_new, base, parts = pl.pallas_call(
        functools.partial(second_kernel, tgt_total, src_total),
        out_shape=[
            jax.ShapeDtypeStruct((1, n_src), f32),
            jax.ShapeDtypeStruct((1, n_tgt), f32),
            jax.ShapeDtypeStruct((ROW, n_tgt), f32),
        ],
        in_specs=[whole, scalar, whole, whole, whole] + [whole] * KEPT,
        out_specs=[whole, whole, whole],
        scratch_shapes=[
            pltpu.VMEM((8, n_src), f32),
            pltpu.VMEM((n_src, 4 * dim), bf16),
            pltpu.VMEM((4 * dim, n_tgt), bf16),
        ],
        compiler_params=params,
        name="second_pass",
    )(lse.reshape(1, n_src), flag, shift, src, tgt, *weights)
    parts = all_to_all(parts.reshape(ROW, 1, n_tgt), "row")
    target_new = base.reshape(n_tgt) - EPS * LN2 * lse_of(parts).reshape(n_tgt)
    return source_new.reshape(n_src), target_new


def solution(mesh):
    return jax.shard_map(
        on_device,
        mesh=mesh,
        in_specs=(P("col", "row"), P("row", "col"), P("col")),
        out_specs=(P("row"), P("col")),
        check_vma=False,
    )
```

profile of v0, /device:TPU:32, one launch (start us, length us, event | category | flops | bytes accessed | tf_op | source)
XLA Modules:
  0.0 302.3 jit_solution(16689648424798849796)
XLA Ops:
  0.6 1.6 collective-permute-start.2
  2.2 2.7 collective-permute-start.1
  4.9 1.4 collective-permute-start
  6.5 1.9 collective-permute-start.10
  8.5 0.4 collective-permute-done
  8.9 0.8 pad_maximum_fusion
  9.7 1.7 collective-permute-start.5
  11.3 2.9 collective-permute-start.4
  14.2 1.3 collective-permute-start.3
  15.6 1.9 collective-permute-start.11
  17.5 1.7 collective-permute-start.8
  19.2 0.8 concatenate.8.src_near
  20.2 1.2 collective-permute-done.11.refs_6_
  21.4 0.8 collective-permute-start.12
  22.5 2.3 collective-permute-start.9
  24.7 2.1 collective-permute-done.12.refs_5_
  27.0 5.3 %collective-permute-done.13.refs_4_ = bf16[8,4096]{1,0:T(8,128)(2,1)S(1)} collective-permute-done((bf16[8,4096]{1,0:T(8,128)(2,1)S(1)}, bf16[8,4096]{1,0:T(8,128)(2,1)S(1)}, u32[]{:S(2)}, u32[]{:S(2)}) %collective-permute-start.13) | collective-permute-done | bytes 65568 | tf_op jit(solution)/shard_map/ppermute | solution.py:165
  32.3 0.8 copy-done
  33.2 0.7 copy-done.1
  33.9 11.3 %first_pass.1 = (bf16[512,4096]{1,0:T(8,128)(2,1)S(1)}, bf16[512,4096]{1,0:T(8,128)(2,1)S(1)}, bf16[512,4096]{1,0:T(8,128)(2,1)S(1)}, bf16[512,4096]{1,0:T(8,128...) custom-call(bf16[64,64]{1,0:T(8,128)(2,1)S(1)} %fusion.20.order, ...), custom_call_target="tpu_custom_call" | custom-call | tf_op jit(solution)/shard_map/first_pass/pallas_call | solution.py:229
  45.3 1.2 collective-permute-done.14
  46.5 104.6 %collective-permute-start.17 = (f32[4096]{0:T(1024)S(1)}, f32[4096]{0:T(1024)S(1)}, u32[]{:S(2)}, u32[]{:S(2)}) collective-permute-start(f32[4096]{0:T(1024)S(1)} %multiply_add_fusion.2), channel_id=1, source_target_pairs={{24,0},{25,1},{26,2},{27,3},{28,4},{29,5},{30,6},{31,7},{0,8},{1,9... | collective-permute-start | bytes 49160 | tf_op jit(solution)/shard_map/ppermute | solution.py:175
  151.1 2.2 collective-permute-start.15
  153.3 1.6 collective-permute-done.16
  154.8 1.5 collective-permute-done.15
  156.4 3.4 %collective-permute-start.20 = (f32[4096]{0:T(1024)S(1)}, f32[4096]{0:T(1024)S(1)}, u32[]{:S(2)}, u32[]{:S(2)}) collective-permute-start(f32[4096]{0:T(1024)S(1)} %multiply_add_fusion.1), channel_id=1, source_target_pairs={{6,0},{7,1},{0,2},{1,3},{2,4},{3,5},{4,6},{5,7},{14,8},{15,9},{8,1... | collective-permute-start | bytes 49160 | tf_op jit(solution)/shard_map/ppermute | solution.py:175
  159.8 2.2 collective-permute-start.18
  161.9 1.6 collective-permute-done.19
  163.5 1.5 collective-permute-done.18
  165.0 118.5 %second_pass.1 = (f32[1,4096]{1,0:T(1,128)}, f32[1,4096]{1,0:T(1,128)S(1)}, f32[8,4096]{1,0:T(8,128)S(1)}) custom-call(f32[1,4096]{1,0:T(1,128)S(1)} %bitcast.7, s32[1,1]{1,0:T(1,128)} %get-tuple-element.19.flag, f32[1,4096]{1,0:T(1,128)S(1)} %get-tuple-element.20.shift, bf16[64,4096]{1,0:T(8,128)(2,1)S(1)} %get-tuple-element.21.src, ...), custom_call_target="tpu_custom_call" | custom-call | tf_op jit(solution)/shard_map/second_pass/pallas_call | solution.py:250
  283.7 17.8 %all_to_all.5 = f32[8,1,4096]{2,1,0:T(1,128)S(1)} all-to-all(f32[8,1,4096]{2,1,0:T(1,128)S(1)} %copy.6), channel_id=1, replica_groups=mesh['row'=8,'col'=32] {'row'}, dimensions={0} | all-to-all | bytes 262144 | tf_op jit(solution)/shard_map/all_to_all | solution.py:190
  301.7 0.6 multiply_subtract_fusion
  (35 shorter events, 1.3 us)
Async XLA Ops:
  0.6 7.8 %collective-permute-start.2 = (bf16[2,4096]{1,0:T(2,128)(2,1)}, bf16[2,4096]{1,0:T(2,128)(2,1)S(1)}, u32[]{:S(2)}, u32[]{:S(2)}) collective-permute-start(bf16[2,4096]{1,0:T(2,128)(2,1)} %param.3), channel_id=1, source_target_pairs={{24,0},{25,1},{26,2},{27,3},{28,4},{29,5},{30,6},{31,7},{0,8},{1,9... | collective-permute-start | bytes 49160 | tf_op jit(solution)/shard_map/ppermute | solution.py:175
  2.2 6.3 %collective-permute-start.1 = (bf16[2,4096]{1,0:T(2,128)(2,1)}, bf16[2,4096]{1,0:T(2,128)(2,1)S(1)}, u32[]{:S(2)}, u32[]{:S(2)}) collective-permute-start(bf16[2,4096]{1,0:T(2,128)(2,1)} %param.3), channel_id=1, source_target_pairs={{16,0},{17,1},{18,2},{19,3},{20,4},{21,5},{22,6},{23,7},{24,8},{25... | collective-permute-start | bytes 49160 | tf_op jit(solution)/shard_map/ppermute | solution.py:175
  4.9 3.9 %collective-permute-start = (bf16[2,4096]{1,0:T(2,128)(2,1)}, bf16[2,4096]{1,0:T(2,128)(2,1)S(1)}, u32[]{:S(2)}, u32[]{:S(2)}) collective-permute-start(bf16[2,4096]{1,0:T(2,128)(2,1)} %param.3), channel_id=1, source_target_pairs={{8,0},{9,1},{10,2},{11,3},{12,4},{13,5},{14,6},{15,7},{16,8},{17,9... | collective-permute-start | bytes 49160 | tf_op jit(solution)/shard_map/ppermute | solution.py:175
  6.4 11.1 %collective-permute-start.7 = (bf16[8,4096]{1,0:T(8,128)(2,1)}, bf16[8,4096]{1,0:T(8,128)(2,1)S(1)}, u32[]{:S(2)}, u32[]{:S(2)}) collective-permute-start(bf16[8,4096]{1,0:T(8,128)(2,1)} %refs_0_.1), channel_id=1, source_target_pairs={{32,0},{64,32},{96,64},{128,96},{160,128},{192,160},{224,192},{0,2... | collective-permute-start | bytes 196616 | tf_op jit(solution)/shard_map/ppermute | solution.py:165
  6.5 9.1 %collective-permute-start.10 = (bf16[8,4096]{1,0:T(8,128)(2,1)}, bf16[8,4096]{1,0:T(8,128)(2,1)S(1)}, u32[]{:S(2)}, u32[]{:S(2)}) collective-permute-start(bf16[8,4096]{1,0:T(8,128)(2,1)} %refs_0_.1), channel_id=1, source_target_pairs={{224,0},{0,32},{32,64},{64,96},{96,128},{128,160},{160,192},{192,2... | collective-permute-start | bytes 196616 | tf_op jit(solution)/shard_map/ppermute | solution.py:165
  9.7 9.5 %collective-permute-start.5 = (bf16[8,4096]{1,0:T(8,128)(2,1)S(1)}, bf16[8,4096]{1,0:T(8,128)(2,1)S(1)}, u32[]{:S(2)}, u32[]{:S(2)}) collective-permute-start(bf16[8,4096]{1,0:T(8,128)(2,1)S(1)} %pad_maximum_fusion), channel_id=1, source_target_pairs={{6,0},{7,1},{0,2},{1,3},{2,4},{3,5},{4,6},{5,7},{14,8},{15,9},{8,1... | collective-permute-start | bytes 196616 | tf_op jit(solution)/shard_map/ppermute | solution.py:175
  11.3 7.9 %collective-permute-start.4 = (bf16[8,4096]{1,0:T(8,128)(2,1)S(1)}, bf16[8,4096]{1,0:T(8,128)(2,1)S(1)}, u32[]{:S(2)}, u32[]{:S(2)}) collective-permute-start(bf16[8,4096]{1,0:T(8,128)(2,1)S(1)} %pad_maximum_fusion), channel_id=1, source_target_pairs={{4,0},{5,1},{6,2},{7,3},{0,4},{1,5},{2,6},{3,7},{12,8},{13,9},{14,... | collective-permute-start | bytes 196616 | tf_op jit(solution)/shard_map/ppermute | solution.py:175
  14.2 5.0 %collective-permute-start.3 = (bf16[8,4096]{1,0:T(8,128)(2,1)S(1)}, bf16[8,4096]{1,0:T(8,128)(2,1)S(1)}, u32[]{:S(2)}, u32[]{:S(2)}) collective-permute-start(bf16[8,4096]{1,0:T(8,128)(2,1)S(1)} %pad_maximum_fusion), channel_id=1, source_target_pairs={{2,0},{3,1},{4,2},{5,3},{6,4},{7,5},{0,6},{1,7},{10,8},{11,9},{12,... | collective-permute-start | bytes 196616 | tf_op jit(solution)/shard_map/ppermute | solution.py:175
  15.6 5.8 %collective-permute-start.11 = (bf16[8,4096]{1,0:T(8,128)(2,1)S(1)}, bf16[8,4096]{1,0:T(8,128)(2,1)S(1)}, u32[]{:S(2)}, u32[]{:S(2)}) collective-permute-start(bf16[8,4096]{1,0:T(8,128)(2,1)S(1)} %collective-permute-done.10.refs_7_), channel_id=1, source_target_pairs={{224,0},{0,32},{32,64},{64,96},{96,128},{128,160},{160,192},{192,2... | collective-permute-start | bytes 196616 | tf_op jit(solution)/shard_map/ppermute | solution.py:165
  17.5 5.0 %collective-permute-start.8 = (bf16[8,4096]{1,0:T(8,128)(2,1)S(1)}, bf16[8,4096]{1,0:T(8,128)(2,1)S(1)}, u32[]{:S(2)}, u32[]{:S(2)}) collective-permute-start(bf16[8,4096]{1,0:T(8,128)(2,1)S(1)} %collective-permute-done.7.refs_1_), channel_id=1, source_target_pairs={{32,0},{64,32},{96,64},{128,96},{160,128},{192,160},{224,192},{0,2... | collective-permute-start | bytes 196616 | tf_op jit(solution)/shard_map/ppermute | solution.py:165
  20.1 12.3 %collective-permute-start.6 = (bf16[32,4096]{1,0:T(8,128)(2,1)S(1)}, bf16[32,4096]{1,0:T(8,128)(2,1)S(1)}, u32[]{:S(2)}, u32[]{:S(2)}) collective-permute-start(bf16[32,4096]{1,0:T(8,128)(2,1)S(1)} %concatenate.8.src_near), channel_id=1, source_target_pairs={{1,0},{0,1},{3,2},{2,3},{5,4},{4,5},{7,6},{6,7},{9,8},{8,9},{11,10... | collective-permute-start | bytes 786440 | tf_op jit(solution)/shard_map/ppermute | solution.py:175
  21.4 5.5 %collective-permute-start.12 = (bf16[8,4096]{1,0:T(8,128)(2,1)S(1)}, bf16[8,4096]{1,0:T(8,128)(2,1)S(1)}, u32[]{:S(2)}, u32[]{:S(2)}) collective-permute-start(bf16[8,4096]{1,0:T(8,128)(2,1)S(1)} %collective-permute-done.11.refs_6_), channel_id=1, source_target_pairs={{224,0},{0,32},{32,64},{64,96},{96,128},{128,160},{160,192},{192,2... | collective-permute-start | bytes 196616 | tf_op jit(solution)/shard_map/ppermute | solution.py:165
  22.5 4.6 %collective-permute-start.9 = (bf16[8,4096]{1,0:T(8,128)(2,1)S(1)}, bf16[8,4096]{1,0:T(8,128)(2,1)S(1)}, u32[]{:S(2)}, u32[]{:S(2)}) collective-permute-start(bf16[8,4096]{1,0:T(8,128)(2,1)S(1)} %collective-permute-done.8.refs_2_), channel_id=1, source_target_pairs={{32,0},{64,32},{96,64},{128,96},{160,128},{192,160},{224,192},{0,2... | collective-permute-start | bytes 196616 | tf_op jit(solution)/shard_map/ppermute | solution.py:165
  26.8 5.5 %collective-permute-start.13 = (bf16[8,4096]{1,0:T(8,128)(2,1)S(1)}, bf16[8,4096]{1,0:T(8,128)(2,1)S(1)}, u32[]{:S(2)}, u32[]{:S(2)}) collective-permute-start(bf16[8,4096]{1,0:T(8,128)(2,1)S(1)} %collective-permute-done.12.refs_5_), channel_id=1, source_target_pairs={{224,0},{0,32},{32,64},{64,96},{96,128},{128,160},{160,192},{192,2... | collective-permute-start | bytes 196616 | tf_op jit(solution)/shard_map/ppermute | solution.py:165
  32.3 0.8 copy-start
  33.2 0.7 copy-start.1
  45.2 1.3 collective-permute-start.14
  46.5 106.8 %collective-permute-start.17 = (f32[4096]{0:T(1024)S(1)}, f32[4096]{0:T(1024)S(1)}, u32[]{:S(2)}, u32[]{:S(2)}) collective-permute-start(f32[4096]{0:T(1024)S(1)} %multiply_add_fusion.2), channel_id=1, source_target_pairs={{24,0},{25,1},{26,2},{27,3},{28,4},{29,5},{30,6},{31,7},{0,8},{1,9... | collective-permute-start | bytes 49160 | tf_op jit(solution)/shard_map/ppermute | solution.py:175
  151.1 3.7 %collective-permute-start.16 = (f32[4096]{0:T(1024)S(1)}, f32[4096]{0:T(1024)S(1)}, u32[]{:S(2)}, u32[]{:S(2)}) collective-permute-start(f32[4096]{0:T(1024)S(1)} %multiply_add_fusion.2), channel_id=1, source_target_pairs={{8,0},{9,1},{10,2},{11,3},{12,4},{13,5},{14,6},{15,7},{16,8},{17,9... | collective-permute-start | bytes 49160 | tf_op jit(solution)/shard_map/ppermute | solution.py:175
  151.1 5.2 %collective-permute-start.15 = (f32[4096]{0:T(1024)S(1)}, f32[4096]{0:T(1024)S(1)}, u32[]{:S(2)}, u32[]{:S(2)}) collective-permute-start(f32[4096]{0:T(1024)S(1)} %multiply_add_fusion.2), channel_id=1, source_target_pairs={{16,0},{17,1},{18,2},{19,3},{20,4},{21,5},{22,6},{23,7},{24,8},{25... | collective-permute-start | bytes 49160 | tf_op jit(solution)/shard_map/ppermute | solution.py:175
  156.4 5.5 %collective-permute-start.20 = (f32[4096]{0:T(1024)S(1)}, f32[4096]{0:T(1024)S(1)}, u32[]{:S(2)}, u32[]{:S(2)}) collective-permute-start(f32[4096]{0:T(1024)S(1)} %multiply_add_fusion.1), channel_id=1, source_target_pairs={{6,0},{7,1},{0,2},{1,3},{2,4},{3,5},{4,6},{5,7},{14,8},{15,9},{8,1... | collective-permute-start | bytes 49160 | tf_op jit(solution)/shard_map/ppermute | solution.py:175
  159.8 3.7 %collective-permute-start.19 = (f32[4096]{0:T(1024)S(1)}, f32[4096]{0:T(1024)S(1)}, u32[]{:S(2)}, u32[]{:S(2)}) collective-permute-start(f32[4096]{0:T(1024)S(1)} %multiply_add_fusion.1), channel_id=1, source_target_pairs={{2,0},{3,1},{4,2},{5,3},{6,4},{7,5},{0,6},{1,7},{10,8},{11,9},{12,... | collective-permute-start | bytes 49160 | tf_op jit(solution)/shard_map/ppermute | solution.py:175
  159.8 5.2 %collective-permute-start.18 = (f32[4096]{0:T(1024)S(1)}, f32[4096]{0:T(1024)S(1)}, u32[]{:S(2)}, u32[]{:S(2)}) collective-permute-start(f32[4096]{0:T(1024)S(1)} %multiply_add_fusion.1), channel_id=1, source_target_pairs={{4,0},{5,1},{6,2},{7,3},{0,4},{1,5},{2,6},{3,7},{12,8},{13,9},{14,... | collective-permute-start | bytes 49160 | tf_op jit(solution)/shard_map/ppermute | solution.py:175
where the time goes:
time: 303 us; the launch traced here: 302 us
  starting transfers between devices  133 us (44%)
  Pallas kernels  130 us (43%)
  blocking collectives  17.8 us (6%)
  waiting for transfers between devices  16.8 us (6%)
    ppermute x14, starting transfers between devices, from_col(): return lax.ppermute(v, 'col', pairs)  124 us
    pallas_call x1, Pallas kernels, on_device(): pl.pallas_call(functools.partial(second_kernel, tgt_total, src_total), ou...  119 us
    all_to_all x1, blocking collectives, all_to_all(): return lax.all_to_all(parts, axis, 0, 0, tiled=True)  17.8 us
    pallas_call x1, Pallas kernels, on_device(): pl.pallas_call(first_kernel, out_shape=[*[pltpu.VMEM((n_tgt // KEPT, n_sr...  11.3 us
    ppermute x7, waiting for transfers between devices, from_row(): return lax.ppermute(v, 'row', [((z + k) % ROW, z) for z in range(ROW)])  8.99 us
    ppermute x7, starting transfers between devices, from_row(): return lax.ppermute(v, 'row', [((z + k) % ROW, z) for z in range(ROW)])  8.69 us
    ppermute x14, waiting for transfers between devices, from_col(): return lax.ppermute(v, 'col', pairs)  7.78 us
  transfers between devices with their start and end apart: 21, of which 11 were waited for; matrix products, arithmetic and copies ran while one was open for 1% of the time, Pallas kernels for 0%

commit v1 on v0

--- a/solution.py
+++ b/solution.py
@@ -26,17 +26,22 @@
     return hi, mid, low
 
 
-def fill_operands(streamed, fixed, bias, lhs, rhs):
-    d, n = streamed.shape
+def fill_streamed(points, bias, lhs):
+    d, n = points.shape
     hi, mid, low = split3(bias)
     row = lax.broadcasted_iota(jnp.int32, (d, n), 0)
     rows = jnp.where(row == 0, hi.astype(jnp.float32), 0.0)
     rows = jnp.where(row == 1, mid.astype(jnp.float32), rows)
     rows = jnp.where(row == 2, low.astype(jnp.float32), rows)
-    points = streamed.astype(jnp.float32)
+    points = points.astype(jnp.float32)
     lhs[:, : 2 * d] = jnp.concatenate([points, rows], axis=0).T.astype(jnp.bfloat16)
     lhs[:, 2 * d :] = jnp.concatenate([points, points], axis=0).T.astype(jnp.bfloat16)
-    hi, mid, low = split3(fixed.astype(jnp.float32) * (2.0 * KAPPA))
+
+
+def fill_fixed(points, rhs):
+    d, n = points.shape
+    row = lax.broadcasted_iota(jnp.int32, (d, n), 0)
+    hi, mid, low = split3(points.astype(jnp.float32) * (2.0 * KAPPA))
     rhs[:d] = hi
     rhs[d : 2 * d] = jnp.where(row < 3, 1.0, 0.0).astype(jnp.bfloat16)
     rhs[2 * d : 3 * d] = mid
@@ -91,16 +96,23 @@
     return jnp.concatenate([piece[...].astype(jnp.float32) for piece in pieces], axis=0)
 
 
-def first_kernel(order, pot, src_near, src_far, *refs):
-    tgt_pieces, weights, (out, shift, flag, src, tgt, lhs, rhs) = refs[: -7 - KEPT], refs[-7 - KEPT : -7], refs[-7:]
+def source_kernel(order, near, far, pot_in, *refs):
+    early, (src, rhs, pot, tgt) = refs[:-4], refs[-4:]
+    features = joined([near, far]).astype(jnp.bfloat16)
+    src[...] = jnp.dot(order[...], features, preferred_element_type=jnp.float32).astype(jnp.bfloat16)
+    fill_fixed(src[...], rhs)
+    pot[...] = KAPPA * pot_in[...]
+    tgt[...] = joined(early)
+
+
+def first_kernel(pot, rhs, early, last, *refs):
+    weights, (out, shift, flag, tgt, lhs) = refs[:KEPT], refs[KEPT:]
     share = weights[0].shape[0]
-    tgt[...] = joined(tgt_pieces).astype(jnp.bfloat16)
-    features = joined([src_near, src_far]).astype(jnp.bfloat16)
-    src[...] = jnp.dot(order[...], features, preferred_element_type=jnp.float32).astype(jnp.bfloat16)
-    bias = KAPPA * (pot[...] - square_norm(tgt[...]))
+    tgt[...] = joined([early, last]).astype(jnp.bfloat16)
+    bias = pot[...] - KAPPA * square_norm(tgt[...])
     offset = jnp.max(bias, axis=1, keepdims=True) - HEAD
     shift[...] = bias - offset
-    fill_operands(tgt[...], src[...], bias - offset, lhs, rhs)
+    fill_streamed(tgt[...], bias - offset, lhs)
 
     def block(step, carry):
         lanes = lanes_of(step, LANES)
@@ -135,18 +147,12 @@
     factors[...] = jnp.broadcast_to(jnp.exp2(bias - top), (8, n_src))
 
     for part in range(KEPT):
-
-        def block(step, carry):
-            rows = lanes_of(step, 128)
-            total = jnp.zeros((16, 8, 128), jnp.float32)
-            for start in range(0, n_src, 128):
-                powers = weights[part][rows, start : start + 128].astype(jnp.float32).reshape(16, 8, 128)
-                total = total + powers * factors[:, start : start + 128][None]
-            sums = total.reshape(128, 128).T.sum(0, keepdims=True)
-            out[:, lanes_of(step + part * (share // 128), 128)] = jnp.broadcast_to(sums, (out.shape[0], 128))
-            return carry
-
-        lax.fori_loop(0, share // 128, block, 0)
+        total = jnp.zeros((share // 8, 8, 128), jnp.float32)
+        for start in range(0, n_src, 128):
+            powers = weights[part][:, start : start + 128].astype(jnp.float32).reshape(share // 8, 8, 128)
+            total = total + powers * factors[:, start : start + 128][None]
+        sums = total.reshape(share, 128).T.sum(0, keepdims=True)
+        out[:, part * share : (part + 1) * share] = jnp.broadcast_to(sums, (out.shape[0], share))
     sums = out[...]
     good = jnp.logical_and(in_range(sums), jnp.min(bias) - jnp.max(bias) > -120.0)
     good = jnp.logical_and(good, flag[0, 0] == 1)
@@ -154,7 +160,8 @@
 
     @pl.when(jnp.logical_not(good))
     def _():
-        fill_operands(src[...], tgt[...], bias, lhs, rhs)
+        fill_streamed(src[...], bias, lhs)
+        fill_fixed(tgt[...], rhs)
         exact_lse(lhs, rhs, out, 0.0)
 
 
@@ -199,7 +206,9 @@
     there = (((x + kx) % X) * Y + (y + ky) % Y) * CORE + (c + kc) % CORE
     src_feature = there * per_src + at % per_src
     at = lax.broadcasted_iota(jnp.int32, (depth, depth), 0)
-    tgt_feature = ((row + at // per_tgt) % ROW) * per_tgt + at % per_tgt
+    piece = at // per_tgt
+    piece = jnp.where(piece < ROW // 2, piece, jnp.where(piece < ROW - 1, piece + 1, ROW // 2))
+    tgt_feature = ((row + piece) % ROW) * per_tgt + at % per_tgt
     return (src_feature == tgt_feature).astype(jnp.bfloat16)
 
 
@@ -221,26 +230,37 @@
     down.append(from_row(down[-1], -1))
     src = jnp.concatenate([src] + [from_col(src, 0, k, 0) for k in range(1, Y)], axis=0)
     far = from_col(src, 0, 0, 1)
-    tgt_pieces = up + down[:0:-1]
+    *early, last = up + down[3:0:-1] + down[4:]
 
     params = pltpu.CompilerParams(vmem_limit_bytes=16 * 2**20)
     f32, bf16 = jnp.float32, jnp.bfloat16
     whole, scalar = pl.BlockSpec(memory_space=pltpu.VMEM), pl.BlockSpec(memory_space=pltpu.SMEM)
-    *weights, lse, shift, flag, src, tgt = pl.pallas_call(
+    src, rhs, pot, tgt = pl.pallas_call(
+        source_kernel,
+        out_shape=[
+            jax.ShapeDtypeStruct((dim, n_src), bf16),
+            jax.ShapeDtypeStruct((4 * dim, n_src), bf16),
+            jax.ShapeDtypeStruct((1, n_tgt), f32),
+            jax.ShapeDtypeStruct((dim - per_tgt, n_tgt), f32),
+        ],
+        compiler_params=params,
+        name="sources",
+    )(order, src, far, target_potential.reshape(1, n_tgt), *early)
+
+    *weights, lse, shift, flag, tgt = pl.pallas_call(
         first_kernel,
         out_shape=[
             *[pltpu.VMEM((n_tgt // KEPT, n_src), bf16)] * KEPT,
             jax.ShapeDtypeStruct((1, n_src), f32),
             jax.ShapeDtypeStruct((1, n_tgt), f32),
             jax.ShapeDtypeStruct((1, 1), jnp.int32),
-            jax.ShapeDtypeStruct((dim, n_src), bf16),
             jax.ShapeDtypeStruct((dim, n_tgt), bf16),
         ],
-        out_specs=[whole] * KEPT + [whole, whole, scalar, whole, whole],
-        scratch_shapes=[pltpu.VMEM((n_tgt, 4 * dim), bf16), pltpu.VMEM((4 * dim, n_src), bf16)],
+        out_specs=[whole] * KEPT + [whole, whole, scalar, whole],
+        scratch_shapes=[pltpu.VMEM((n_tgt, 4 * dim), bf16)],
         compiler_params=params,
         name="first_pass",
-    )(order, target_potential.reshape(1, n_tgt), src, far, *tgt_pieces)
+    )(pot, rhs, tgt, last)
 
     lse = lse.reshape(n_src)
     lse = pair_lse(lse, from_col(lse, 0, 0, 1))

time: 303 us -> 302 us (level)
  starting transfers between devices: 133 us -> 138 us
    ppermute x14, starting transfers between devices: 124 us -> 129 us  [from_col(): return lax.ppermute(v, 'col', pairs)]
    pallas_call x1, Pallas kernels: 119 us -> 115 us  [on_device(): pl.pallas_call(functools.partial(second_kernel, tgt_total, src_total), ou...]
where the time goes in v1:
time: 302 us; the launch traced here: 300 us
  starting transfers between devices  138 us (46%)
  Pallas kernels  127 us (42%)
  blocking collectives  15.8 us (5%)
  waiting for transfers between devices  14.3 us (5%)
    ppermute x14, starting transfers between devices, from_col(): return lax.ppermute(v, 'col', pairs)  129 us
    pallas_call x1, Pallas kernels, on_device(): pl.pallas_call(functools.partial(second_kernel, tgt_total, src_total), ou...  115 us
    all_to_all x1, blocking collectives, all_to_all(): return lax.all_to_all(parts, axis, 0, 0, tiled=True)  15.8 us
    pallas_call x1, Pallas kernels, on_device(): pl.pallas_call(first_kernel, out_shape=[*[pltpu.VMEM((n_tgt // KEPT, n_sr...  11 us
    ppermute x7, starting transfers between devices, from_row(): return lax.ppermute(v, 'row', [((z + k) % ROW, z) for z in range(ROW)])  8.69 us
    ppermute x14, waiting for transfers between devices, from_col(): return lax.ppermute(v, 'col', pairs)  7.45 us
    ppermute x7, waiting for transfers between devices, from_row(): return lax.ppermute(v, 'row', [((z + k) % ROW, z) for z in range(ROW)])  6.88 us
  transfers between devices with their start and end apart: 21, of which 11 were waited for; matrix products, arithmetic and copies ran while one was open for 1% of the time, Pallas kernels for 0%

profile of v1, /device:TPU:32, one launch (start us, length us, event | category | flops | bytes accessed | tf_op | source)
XLA Modules:
  0.0 299.8 jit_solution(10453817709639137105)
XLA Ops:
  0.6 1.6 collective-permute-start.2
  2.2 2.7 collective-permute-start.1
  4.9 1.4 collective-permute-start
  6.5 1.9 collective-permute-start.10
  8.9 0.8 pad_maximum_fusion
  9.7 1.7 collective-permute-start.5
  11.3 2.9 collective-permute-start.4
  14.2 1.3 collective-permute-start.3
  15.6 1.9 collective-permute-start.11
  17.5 1.7 collective-permute-start.8
  19.2 0.8 concatenate.8.near
  20.2 1.2 collective-permute-done.11.refs_5_
  21.4 0.8 collective-permute-start.12
  22.5 2.3 collective-permute-start.9
  24.7 2.1 collective-permute-done.12.refs_4_
  27.0 0.8 copy-done
  27.9 0.7 copy-done.1
  29.2 3.2 %collective-permute-done.13.last = bf16[8,4096]{1,0:T(8,128)(2,1)S(1)} collective-permute-done((bf16[8,4096]{1,0:T(8,128)(2,1)S(1)}, bf16[8,4096]{1,0:T(8,128)(2,1)S(1)}, u32[]{:S(2)}, u32[]{:S(2)}) %collective-permute-start.13) | collective-permute-done | bytes 65568 | tf_op jit(solution)/shard_map/ppermute | solution.py:172
  32.3 11.0 %first_pass.1 = (bf16[512,4096]{1,0:T(8,128)(2,1)S(1)}, bf16[512,4096]{1,0:T(8,128)(2,1)S(1)}, bf16[512,4096]{1,0:T(8,128)(2,1)S(1)}, bf16[512,4096]{1,0:T(8,128...) custom-call(f32[1,4096]{1,0:T(1,128)S(1)} %get-tuple-element.21.pot,, ...), custom_call_target="tpu_custom_call" | custom-call | tf_op jit(solution)/shard_map/first_pass/pallas_call | solution.py:250
  43.4 105.8 %collective-permute-start.14 = (f32[4096]{0:T(1024)S(1)}, f32[4096]{0:T(1024)S(1)}, u32[]{:S(2)}, u32[]{:S(2)}) collective-permute-start(f32[4096]{0:T(1024)S(1)} %bitcast.9), channel_id=1, source_target_pairs={{1,0},{0,1},{3,2},{2,3},{5,4},{4,5},{7,6},{6,7},{9,8},{8,9},{11,10... | collective-permute-start | bytes 49160 | tf_op jit(solution)/shard_map/ppermute | solution.py:182
  149.2 0.8 collective-permute-done.14
  150.1 3.8 %collective-permute-start.17 = (f32[4096]{0:T(1024)S(1)}, f32[4096]{0:T(1024)S(1)}, u32[]{:S(2)}, u32[]{:S(2)}) collective-permute-start(f32[4096]{0:T(1024)S(1)} %multiply_add_fusion.2), channel_id=1, source_target_pairs={{24,0},{25,1},{26,2},{27,3},{28,4},{29,5},{30,6},{31,7},{0,8},{1,9... | collective-permute-start | bytes 49160 | tf_op jit(solution)/shard_map/ppermute | solution.py:182
  153.8 2.2 collective-permute-start.15
  156.0 1.6 collective-permute-done.16
  157.5 1.5 collective-permute-done.15
  159.1 3.4 %collective-permute-start.20 = (f32[4096]{0:T(1024)S(1)}, f32[4096]{0:T(1024)S(1)}, u32[]{:S(2)}, u32[]{:S(2)}) collective-permute-start(f32[4096]{0:T(1024)S(1)} %multiply_add_fusion.1), channel_id=1, source_target_pairs={{6,0},{7,1},{0,2},{1,3},{2,4},{3,5},{4,6},{5,7},{14,8},{15,9},{8,1... | collective-permute-start | bytes 49160 | tf_op jit(solution)/shard_map/ppermute | solution.py:182
  162.5 2.2 collective-permute-start.18
  164.6 1.6 collective-permute-done.19
  166.2 1.5 collective-permute-done.18
  167.8 115.3 %second_pass.1 = (f32[1,4096]{1,0:T(1,128)}, f32[1,4096]{1,0:T(1,128)S(1)}, f32[8,4096]{1,0:T(8,128)S(1)}) custom-call(f32[1,4096]{1,0:T(1,128)S(1)} %bitcast.7, s32[1,1]{1,0:T(1,128)} %get-tuple-element.25.flag, f32[1,4096]{1,0:T(1,128)S(1)} %get-tuple-element.26.shift, bf16[64,4096]{1,0:T(8,128)(2,1)S(1)} %get-tuple-element.27.src, ...), custom_call_target="tpu_custom_call" | custom-call | tf_op jit(solution)/shard_map/second_pass/pallas_call | solution.py:270
  283.2 15.8 %all_to_all.5 = f32[8,1,4096]{2,1,0:T(1,128)S(1)} all-to-all(f32[8,1,4096]{2,1,0:T(1,128)S(1)} %copy.6), channel_id=1, replica_groups=mesh['row'=8,'col'=32] {'row'}, dimensions={0} | all-to-all | bytes 262144 | tf_op jit(solution)/shard_map/all_to_all | solution.py:197
  299.2 0.6 multiply_subtract_fusion
  (36 shorter events, 2.2 us)
Async XLA Ops:
  0.6 7.8 %collective-permute-start.2 = (bf16[2,4096]{1,0:T(2,128)(2,1)}, bf16[2,4096]{1,0:T(2,128)(2,1)S(1)}, u32[]{:S(2)}, u32[]{:S(2)}) collective-permute-start(bf16[2,4096]{1,0:T(2,128)(2,1)} %param.3), channel_id=1, source_target_pairs={{24,0},{25,1},{26,2},{27,3},{28,4},{29,5},{30,6},{31,7},{0,8},{1,9... | collective-permute-start | bytes 49160 | tf_op jit(solution)/shard_map/ppermute | solution.py:182
  2.2 6.3 %collective-permute-start.1 = (bf16[2,4096]{1,0:T(2,128)(2,1)}, bf16[2,4096]{1,0:T(2,128)(2,1)S(1)}, u32[]{:S(2)}, u32[]{:S(2)}) collective-permute-start(bf16[2,4096]{1,0:T(2,128)(2,1)} %param.3), channel_id=1, source_target_pairs={{16,0},{17,1},{18,2},{19,3},{20,4},{21,5},{22,6},{23,7},{24,8},{25... | collective-permute-start | bytes 49160 | tf_op jit(solution)/shard_map/ppermute | solution.py:182
  4.9 3.9 %collective-permute-start = (bf16[2,4096]{1,0:T(2,128)(2,1)}, bf16[2,4096]{1,0:T(2,128)(2,1)S(1)}, u32[]{:S(2)}, u32[]{:S(2)}) collective-permute-start(bf16[2,4096]{1,0:T(2,128)(2,1)} %param.3), channel_id=1, source_target_pairs={{8,0},{9,1},{10,2},{11,3},{12,4},{13,5},{14,6},{15,7},{16,8},{17,9... | collective-permute-start | bytes 49160 | tf_op jit(solution)/shard_map/ppermute | solution.py:182
  6.4 11.1 %collective-permute-start.7 = (bf16[8,4096]{1,0:T(8,128)(2,1)}, bf16[8,4096]{1,0:T(8,128)(2,1)S(1)}, u32[]{:S(2)}, u32[]{:S(2)}) collective-permute-start(bf16[8,4096]{1,0:T(8,128)(2,1)} %refs_0_.1), channel_id=1, source_target_pairs={{32,0},{64,32},{96,64},{128,96},{160,128},{192,160},{224,192},{0,2... | collective-permute-start | bytes 196616 | tf_op jit(solution)/shard_map/ppermute | solution.py:172
  6.5 9.1 %collective-permute-start.10 = (bf16[8,4096]{1,0:T(8,128)(2,1)}, bf16[8,4096]{1,0:T(8,128)(2,1)S(1)}, u32[]{:S(2)}, u32[]{:S(2)}) collective-permute-start(bf16[8,4096]{1,0:T(8,128)(2,1)} %refs_0_.1), channel_id=1, source_target_pairs={{224,0},{0,32},{32,64},{64,96},{96,128},{128,160},{160,192},{192,2... | collective-permute-start | bytes 196616 | tf_op jit(solution)/shard_map/ppermute | solution.py:172
  9.7 9.5 %collective-permute-start.5 = (bf16[8,4096]{1,0:T(8,128)(2,1)S(1)}, bf16[8,4096]{1,0:T(8,128)(2,1)S(1)}, u32[]{:S(2)}, u32[]{:S(2)}) collective-permute-start(bf16[8,4096]{1,0:T(8,128)(2,1)S(1)} %pad_maximum_fusion), channel_id=1, source_target_pairs={{6,0},{7,1},{0,2},{1,3},{2,4},{3,5},{4,6},{5,7},{14,8},{15,9},{8,1... | collective-permute-start | bytes 196616 | tf_op jit(solution)/shard_map/ppermute | solution.py:182
  11.3 7.9 %collective-permute-start.4 = (bf16[8,4096]{1,0:T(8,128)(2,1)S(1)}, bf16[8,4096]{1,0:T(8,128)(2,1)S(1)}, u32[]{:S(2)}, u32[]{:S(2)}) collective-permute-start(bf16[8,4096]{1,0:T(8,128)(2,1)S(1)} %pad_maximum_fusion), channel_id=1, source_target_pairs={{4,0},{5,1},{6,2},{7,3},{0,4},{1,5},{2,6},{3,7},{12,8},{13,9},{14,... | collective-permute-start | bytes 196616 | tf_op jit(solution)/shard_map/ppermute | solution.py:182
  14.2 5.0 %collective-permute-start.3 = (bf16[8,4096]{1,0:T(8,128)(2,1)S(1)}, bf16[8,4096]{1,0:T(8,128)(2,1)S(1)}, u32[]{:S(2)}, u32[]{:S(2)}) collective-permute-start(bf16[8,4096]{1,0:T(8,128)(2,1)S(1)} %pad_maximum_fusion), channel_id=1, source_target_pairs={{2,0},{3,1},{4,2},{5,3},{6,4},{7,5},{0,6},{1,7},{10,8},{11,9},{12,... | collective-permute-start | bytes 196616 | tf_op jit(solution)/shard_map/ppermute | solution.py:182
  15.6 5.8 %collective-permute-start.11 = (bf16[8,4096]{1,0:T(8,128)(2,1)S(1)}, bf16[8,4096]{1,0:T(8,128)(2,1)S(1)}, u32[]{:S(2)}, u32[]{:S(2)}) collective-permute-start(bf16[8,4096]{1,0:T(8,128)(2,1)S(1)} %collective-permute-done.10.refs_6_), channel_id=1, source_target_pairs={{224,0},{0,32},{32,64},{64,96},{96,128},{128,160},{160,192},{192,2... | collective-permute-start | bytes 196616 | tf_op jit(solution)/shard_map/ppermute | solution.py:172
  17.5 5.0 %collective-permute-start.8 = (bf16[8,4096]{1,0:T(8,128)(2,1)S(1)}, bf16[8,4096]{1,0:T(8,128)(2,1)S(1)}, u32[]{:S(2)}, u32[]{:S(2)}) collective-permute-start(bf16[8,4096]{1,0:T(8,128)(2,1)S(1)} %collective-permute-done.7.refs_1_), channel_id=1, source_target_pairs={{32,0},{64,32},{96,64},{128,96},{160,128},{192,160},{224,192},{0,2... | collective-permute-start | bytes 196616 | tf_op jit(solution)/shard_map/ppermute | solution.py:172
  20.1 7.0 %collective-permute-start.6 = (bf16[32,4096]{1,0:T(8,128)(2,1)S(1)}, bf16[32,4096]{1,0:T(8,128)(2,1)S(1)}, u32[]{:S(2)}, u32[]{:S(2)}) collective-permute-start(bf16[32,4096]{1,0:T(8,128)(2,1)S(1)} %concatenate.8.near), channel_id=1, source_target_pairs={{1,0},{0,1},{3,2},{2,3},{5,4},{4,5},{7,6},{6,7},{9,8},{8,9},{11,10... | collective-permute-start | bytes 786440 | tf_op jit(solution)/shard_map/ppermute | solution.py:182
  21.4 5.5 %collective-permute-start.12 = (bf16[8,4096]{1,0:T(8,128)(2,1)S(1)}, bf16[8,4096]{1,0:T(8,128)(2,1)S(1)}, u32[]{:S(2)}, u32[]{:S(2)}) collective-permute-start(bf16[8,4096]{1,0:T(8,128)(2,1)S(1)} %collective-permute-done.11.refs_5_), channel_id=1, source_target_pairs={{224,0},{0,32},{32,64},{64,96},{96,128},{128,160},{160,192},{192,2... | collective-permute-start | bytes 196616 | tf_op jit(solution)/shard_map/ppermute | solution.py:172
  22.5 4.6 %collective-permute-start.9 = (bf16[8,4096]{1,0:T(8,128)(2,1)S(1)}, bf16[8,4096]{1,0:T(8,128)(2,1)S(1)}, u32[]{:S(2)}, u32[]{:S(2)}) collective-permute-start(bf16[8,4096]{1,0:T(8,128)(2,1)S(1)} %collective-permute-done.8.refs_2_), channel_id=1, source_target_pairs={{32,0},{64,32},{96,64},{128,96},{160,128},{192,160},{224,192},{0,2... | collective-permute-start | bytes 196616 | tf_op jit(solution)/shard_map/ppermute | solution.py:172
  26.8 5.5 %collective-permute-start.13 = (bf16[8,4096]{1,0:T(8,128)(2,1)S(1)}, bf16[8,4096]{1,0:T(8,128)(2,1)S(1)}, u32[]{:S(2)}, u32[]{:S(2)}) collective-permute-start(bf16[8,4096]{1,0:T(8,128)(2,1)S(1)} %collective-permute-done.12.refs_4_), channel_id=1, source_target_pairs={{224,0},{0,32},{32,64},{64,96},{96,128},{128,160},{160,192},{192,2... | collective-permute-start | bytes 196616 | tf_op jit(solution)/shard_map/ppermute | solution.py:172
  27.0 0.8 copy-start
  27.9 0.7 copy-start.1
  43.4 106.7 %collective-permute-start.14 = (f32[4096]{0:T(1024)S(1)}, f32[4096]{0:T(1024)S(1)}, u32[]{:S(2)}, u32[]{:S(2)}) collective-permute-start(f32[4096]{0:T(1024)S(1)} %bitcast.9), channel_id=1, source_target_pairs={{1,0},{0,1},{3,2},{2,3},{5,4},{4,5},{7,6},{6,7},{9,8},{8,9},{11,10... | collective-permute-start | bytes 49160 | tf_op jit(solution)/shard_map/ppermute | solution.py:182
  150.1 5.9 %collective-permute-start.17 = (f32[4096]{0:T(1024)S(1)}, f32[4096]{0:T(1024)S(1)}, u32[]{:S(2)}, u32[]{:S(2)}) collective-permute-start(f32[4096]{0:T(1024)S(1)} %multiply_add_fusion.2), channel_id=1, source_target_pairs={{24,0},{25,1},{26,2},{27,3},{28,4},{29,5},{30,6},{31,7},{0,8},{1,9... | collective-permute-start | bytes 49160 | tf_op jit(solution)/shard_map/ppermute | solution.py:182
  153.8 3.7 %collective-permute-start.16 = (f32[4096]{0:T(1024)S(1)}, f32[4096]{0:T(1024)S(1)}, u32[]{:S(2)}, u32[]{:S(2)}) collective-permute-start(f32[4096]{0:T(1024)S(1)} %multiply_add_fusion.2), channel_id=1, source_target_pairs={{8,0},{9,1},{10,2},{11,3},{12,4},{13,5},{14,6},{15,7},{16,8},{17,9... | collective-permute-start | bytes 49160 | tf_op jit(solution)/shard_map/ppermute | solution.py:182
  153.8 5.2 %collective-permute-start.15 = (f32[4096]{0:T(1024)S(1)}, f32[4096]{0:T(1024)S(1)}, u32[]{:S(2)}, u32[]{:S(2)}) collective-permute-start(f32[4096]{0:T(1024)S(1)} %multiply_add_fusion.2), channel_id=1, source_target_pairs={{16,0},{17,1},{18,2},{19,3},{20,4},{21,5},{22,6},{23,7},{24,8},{25... | collective-permute-start | bytes 49160 | tf_op jit(solution)/shard_map/ppermute | solution.py:182
  159.1 5.6 %collective-permute-start.20 = (f32[4096]{0:T(1024)S(1)}, f32[4096]{0:T(1024)S(1)}, u32[]{:S(2)}, u32[]{:S(2)}) collective-permute-start(f32[4096]{0:T(1024)S(1)} %multiply_add_fusion.1), channel_id=1, source_target_pairs={{6,0},{7,1},{0,2},{1,3},{2,4},{3,5},{4,6},{5,7},{14,8},{15,9},{8,1... | collective-permute-start | bytes 49160 | tf_op jit(solution)/shard_map/ppermute | solution.py:182
  162.5 3.7 %collective-permute-start.19 = (f32[4096]{0:T(1024)S(1)}, f32[4096]{0:T(1024)S(1)}, u32[]{:S(2)}, u32[]{:S(2)}) collective-permute-start(f32[4096]{0:T(1024)S(1)} %multiply_add_fusion.1), channel_id=1, source_target_pairs={{2,0},{3,1},{4,2},{5,3},{6,4},{7,5},{0,6},{1,7},{10,8},{11,9},{12,... | collective-permute-start | bytes 49160 | tf_op jit(solution)/shard_map/ppermute | solution.py:182
  162.5 5.2 %collective-permute-start.18 = (f32[4096]{0:T(1024)S(1)}, f32[4096]{0:T(1024)S(1)}, u32[]{:S(2)}, u32[]{:S(2)}) collective-permute-start(f32[4096]{0:T(1024)S(1)} %multiply_add_fusion.1), channel_id=1, source_target_pairs={{4,0},{5,1},{6,2},{7,3},{0,4},{1,5},{2,6},{3,7},{12,8},{13,9},{14,... | collective-permute-start | bytes 49160 | tf_op jit(solution)/shard_map/ppermute | solution.py:182

commit v2 on v1

--- a/solution.py
+++ b/solution.py
@@ -12,7 +12,7 @@
 LN2 = math.log(2.0)
 KAPPA = 1.0 / (EPS * LN2)
 ROWS = 128
-LANES = 1024
+LANES = 4096
 EXACT_LANES = 256
 KEPT = 8
 HEAD = 40.0
@@ -96,20 +96,13 @@
     return jnp.concatenate([piece[...].astype(jnp.float32) for piece in pieces], axis=0)
 
 
-def source_kernel(order, near, far, pot_in, *refs):
-    early, (src, rhs, pot, tgt) = refs[:-4], refs[-4:]
+def first_kernel(order, near, far, tgt, pot, *refs):
+    weights, (out, shift, flag, src, lhs, rhs) = refs[:KEPT], refs[KEPT:]
+    share = weights[0].shape[0]
     features = joined([near, far]).astype(jnp.bfloat16)
     src[...] = jnp.dot(order[...], features, preferred_element_type=jnp.float32).astype(jnp.bfloat16)
     fill_fixed(src[...], rhs)
-    pot[...] = KAPPA * pot_in[...]
-    tgt[...] = joined(early)
-
-
-def first_kernel(pot, rhs, early, last, *refs):
-    weights, (out, shift, flag, tgt, lhs) = refs[:KEPT], refs[KEPT:]
-    share = weights[0].shape[0]
-    tgt[...] = joined([early, last]).astype(jnp.bfloat16)
-    bias = pot[...] - KAPPA * square_norm(tgt[...])
+    bias = KAPPA * (pot[...] - square_norm(tgt[...]))
     offset = jnp.max(bias, axis=1, keepdims=True) - HEAD
     shift[...] = bias - offset
     fill_streamed(tgt[...], bias - offset, lhs)
@@ -188,9 +181,9 @@
 
 
 def ring_lse(own, others):
-    top = jnp.maximum(jnp.maximum(own, others[1]), jnp.maximum(others[0], others[2]))
+    top = jnp.maximum(jnp.maximum(others[0], others[2]), jnp.maximum(own, others[1]))
     near = jnp.exp2(others[0] - top) + jnp.exp2(others[2] - top)
-    return top + jnp.log2((jnp.exp2(own - top) + jnp.exp2(others[1] - top)) + near)
+    return top + jnp.log2(near + (jnp.exp2(own - top) + jnp.exp2(others[1] - top)))
 
 
 def all_to_all(parts, axis):
@@ -206,9 +199,7 @@
     there = (((x + kx) % X) * Y + (y + ky) % Y) * CORE + (c + kc) % CORE
     src_feature = there * per_src + at % per_src
     at = lax.broadcasted_iota(jnp.int32, (depth, depth), 0)
-    piece = at // per_tgt
-    piece = jnp.where(piece < ROW // 2, piece, jnp.where(piece < ROW - 1, piece + 1, ROW // 2))
-    tgt_feature = ((row + piece) % ROW) * per_tgt + at % per_tgt
+    tgt_feature = at
     return (src_feature == tgt_feature).astype(jnp.bfloat16)
 
 
@@ -220,47 +211,36 @@
     dim = per_src * X * Y * CORE
     order = feature_order(per_src, per_tgt)
 
-    up = [target_points]
-    down = [target_points]
     src = source_points
-    src = jnp.concatenate([src] + [from_col(src, k, 0, 0) for k in range(1, X)], axis=0)
-    for _ in range(ROW // 2 - 1):
-        up.append(from_row(up[-1], 1))
-        down.append(from_row(down[-1], -1))
-    down.append(from_row(down[-1], -1))
+    pot = target_potential.reshape(1, n_tgt)
+    copies = jnp.broadcast_to(target_points[None], (ROW,) + target_points.shape)
+
+    tgt = all_to_all(copies, "row")
+    src = jnp.concatenate([src] + [from_col(source_points, k, 0, 0) for k in range(1, X)], axis=0)
     src = jnp.concatenate([src] + [from_col(src, 0, k, 0) for k in range(1, Y)], axis=0)
     far = from_col(src, 0, 0, 1)
-    *early, last = up + down[3:0:-1] + down[4:]
-
-    params = pltpu.CompilerParams(vmem_limit_bytes=16 * 2**20)
+
+    params = pltpu.CompilerParams(vmem_limit_bytes=12 * 2**20)
     f32, bf16 = jnp.float32, jnp.bfloat16
     whole, scalar = pl.BlockSpec(memory_space=pltpu.VMEM), pl.BlockSpec(memory_space=pltpu.SMEM)
-    src, rhs, pot, tgt = pl.pallas_call(
-        source_kernel,
-        out_shape=[
-            jax.ShapeDtypeStruct((dim, n_src), bf16),
-            jax.ShapeDtypeStruct((4 * dim, n_src), bf16),
-            jax.ShapeDtypeStruct((1, n_tgt), f32),
-            jax.ShapeDtypeStruct((dim - per_tgt, n_tgt), f32),
-        ],
-        compiler_params=params,
-        name="sources",
-    )(order, src, far, target_potential.reshape(1, n_tgt), *early)
-
-    *weights, lse, shift, flag, tgt = pl.pallas_call(
+    tgt = tgt.reshape(dim, n_tgt)
+    *weights, lse, shift, flag, src = pl.pallas_call(
         first_kernel,
         out_shape=[
             *[pltpu.VMEM((n_tgt // KEPT, n_src), bf16)] * KEPT,
             jax.ShapeDtypeStruct((1, n_src), f32),
             jax.ShapeDtypeStruct((1, n_tgt), f32),
             jax.ShapeDtypeStruct((1, 1), jnp.int32),
-            jax.ShapeDtypeStruct((dim, n_tgt), bf16),
+            jax.ShapeDtypeStruct((dim, n_src), bf16),
         ],
         out_specs=[whole] * KEPT + [whole, whole, scalar, whole],
-        scratch_shapes=[pltpu.VMEM((n_tgt, 4 * dim), bf16)],
+        scratch_shapes=[
+            pltpu.VMEM((n_tgt, 4 * dim), bf16),
+            pltpu.VMEM((4 * dim, n_src), bf16),
+        ],
         compiler_params=params,
         name="first_pass",
-    )(pot, rhs, tgt, last)
+    )(order, src, far, tgt, pot)
 
     lse = lse.reshape(n_src)
     lse = pair_lse(lse, from_col(lse, 0, 0, 1))

time: 302 us -> 294 us (0.974)
  blocking collectives: 15.8 us -> 10.9 us
    ppermute x7 -> x0, starting transfers between devices: 8.69 us -> none  [from_row(): return lax.ppermute(v, 'row', [((z + k) % ROW, z) for z in range(ROW)])]
    all_to_all x0 -> x1, starting transfers between devices: none -> 8.57 us  [all_to_all(): return lax.all_to_all(parts, axis, 0, 0, tiled=True)]
    ppermute x7 -> x0, waiting for transfers between devices: 6.88 us -> none  [from_row(): return lax.ppermute(v, 'row', [((z + k) % ROW, z) for z in range(ROW)])]
    all_to_all x1, blocking collectives: 15.8 us -> 10.9 us  [all_to_all(): return lax.all_to_all(parts, axis, 0, 0, tiled=True)]
  transfers between devices with their start and end apart: 21 -> 15, of which waited for: 11 -> 7; matrix products, arithmetic and copies ran while one was open for 1% -> 1% of each run, Pallas kernels for 0% -> 0%
where the time goes in v2:
time: 294 us; the launch traced here: 291 us
  starting transfers between devices  137 us (47%)
  Pallas kernels  126 us (43%)
  waiting for transfers between devices  11.5 us (4%)
  blocking collectives  10.9 us (4%)
  local copies, waits for them, and re-layouts  3.35 us (1%)
    ppermute x14, starting transfers between devices, from_col(): return lax.ppermute(v, 'col', pairs)  129 us
    pallas_call x1, Pallas kernels, on_device(): pl.pallas_call(functools.partial(second_kernel, tgt_total, src_total), ou...  115 us
    all_to_all x1, blocking collectives, all_to_all(): return lax.all_to_all(parts, axis, 0, 0, tiled=True)  10.9 us
    pallas_call x1, Pallas kernels, on_device(): pl.pallas_call(first_kernel, out_shape=[*[pltpu.VMEM((n_tgt // KEPT, n_sr...  10.4 us
    ppermute x14, waiting for transfers between devices, from_col(): return lax.ppermute(v, 'col', pairs)  8.61 us
    all_to_all x1, starting transfers between devices, all_to_all(): return lax.all_to_all(parts, axis, 0, 0, tiled=True)  8.57 us
  transfers between devices with their start and end apart: 15, of which 7 were waited for; matrix products, arithmetic and copies ran while one was open for 1% of the time, Pallas kernels for 0%

profile of v2, /device:TPU:32, one launch (start us, length us, event | category | flops | bytes accessed | tf_op | source)
XLA Modules:
  0.0 291.3 jit_solution(12857536877063231847)
XLA Ops:
  0.6 1.6 collective-permute-start.2
  2.2 2.7 collective-permute-start.1
  4.9 1.4 collective-permute-start
  6.4 1.7 broadcast_in_dim.2
  8.0 8.6 %all-to-all-start = ((bf16[8,8,4096]{2,1,0:T(8,128)(2,1)}), bf16[8,8,4096]{2,1,0:T(8,128)(2,1)S(1)}, u32[]{:S(2)}, u32[]{:S(2)}) async-start(bf16[8,8,4096]{2,1,0:T(8,128)(2,1)} %broadcast_in_dim.2), calls=%async_computation | async-start | bytes 1048576 | tf_op jit(solution)/shard_map/all_to_all | solution.py:190
  16.7 0.8 pad_maximum_fusion
  17.5 1.7 collective-permute-start.5
  19.1 2.9 collective-permute-start.4
  22.0 1.3 collective-permute-start.3
  23.4 1.6 collective-permute-done.4
  25.0 1.3 collective-permute-done.3
  26.3 0.8 concatenate.8.near
  27.1 0.3 collective-permute-start.6
  27.5 1.4 collective-permute-done.6.far
  28.9 2.9 all-to-all-done
  31.8 0.7 copy-done
  32.5 10.4 %first_pass.1 = (bf16[512,4096]{1,0:T(8,128)(2,1)S(1)}, bf16[512,4096]{1,0:T(8,128)(2,1)S(1)}, bf16[512,4096]{1,0:T(8,128)(2,1)S(1)}, bf16[512,4096]{1,0:T(8,128...) custom-call(bf16[64,64]{1,0:T(8,128)(2,1)S(1)} %fusion.17.order, ...), custom_call_target="tpu_custom_call" | custom-call | tf_op jit(solution)/shard_map/first_pass/pallas_call | solution.py:227
  42.9 103.4 %collective-permute-start.7 = (f32[4096]{0:T(1024)S(1)}, f32[4096]{0:T(1024)S(1)}, u32[]{:S(2)}, u32[]{:S(2)}) collective-permute-start(f32[4096]{0:T(1024)S(1)} %bitcast.12), channel_id=1, source_target_pairs={{1,0},{0,1},{3,2},{2,3},{5,4},{4,5},{7,6},{6,7},{9,8},{8,9},{11,10... | collective-permute-start | bytes 49160 | tf_op jit(solution)/shard_map/ppermute | solution.py:175
  146.3 0.8 collective-permute-done.7
  147.3 4.2 %collective-permute-start.9 = (f32[4096]{0:T(1024)S(1)}, f32[4096]{0:T(1024)S(1)}, u32[]{:S(2)}, u32[]{:S(2)}) collective-permute-start(f32[4096]{0:T(1024)S(1)} %multiply_add_fusion.2), channel_id=1, source_target_pairs={{24,0},{25,1},{26,2},{27,3},{28,4},{29,5},{30,6},{31,7},{0,8},{1,9... | collective-permute-start | bytes 49160 | tf_op jit(solution)/shard_map/ppermute | solution.py:175
  151.5 2.1 collective-permute-start.8
  153.6 1.7 collective-permute-done.9
  155.4 3.7 %collective-permute-start.13 = (f32[4096]{0:T(1024)S(1)}, f32[4096]{0:T(1024)S(1)}, u32[]{:S(2)}, u32[]{:S(2)}) collective-permute-start(f32[4096]{0:T(1024)S(1)} %multiply_add_fusion.1), channel_id=1, source_target_pairs={{4,0},{5,1},{6,2},{7,3},{0,4},{1,5},{2,6},{3,7},{12,8},{13,9},{14,... | collective-permute-start | bytes 49160 | tf_op jit(solution)/shard_map/ppermute | solution.py:175
  159.1 0.7 collective-permute-start.12
  159.8 2.5 collective-permute-start.11
  162.3 1.7 collective-permute-done.12
  164.1 115.3 %second_pass.1 = (f32[1,4096]{1,0:T(1,128)}, f32[1,4096]{1,0:T(1,128)S(1)}, f32[8,4096]{1,0:T(8,128)S(1)}) custom-call(f32[1,4096]{1,0:T(1,128)S(1)} %bitcast.10, s32[1,1]{1,0:T(1,128)} %get-tuple-element.18.flag, f32[1,4096]{1,0:T(1,128)S(1)} %get-tuple-element.19.shift, bf16[64,4096]{1,0:T(8,128)(2,1)S(1)} %get-tuple-element.20.src, ...), custom_call_target="tpu_custom_call" | custom-call | tf_op jit(solution)/shard_map/second_pass/pallas_call | solution.py:250
  279.3 0.1 copy.6
  279.5 10.9 %all_to_all.10 = f32[8,1,4096]{2,1,0:T(1,128)S(1)} all-to-all(f32[8,1,4096]{2,1,0:T(1,128)S(1)} %copy.6), channel_id=1, replica_groups=mesh['row'=8,'col'=32] {'row'}, dimensions={0} | all-to-all | bytes 262144 | tf_op jit(solution)/shard_map/all_to_all | solution.py:190
  290.4 0.1 reduce_max.9
  290.5 0.1 fusion.2
  290.6 0.6 multiply_subtract_fusion
  (20 shorter events, 0.3 us)
Async XLA Ops:
  0.6 16.0 %collective-permute-start.2 = (bf16[2,4096]{1,0:T(2,128)(2,1)}, bf16[2,4096]{1,0:T(2,128)(2,1)S(1)}, u32[]{:S(2)}, u32[]{:S(2)}) collective-permute-start(bf16[2,4096]{1,0:T(2,128)(2,1)} %param.3), channel_id=1, source_target_pairs={{24,0},{25,1},{26,2},{27,3},{28,4},{29,5},{30,6},{31,7},{0,8},{1,9... | collective-permute-start | bytes 49160 | tf_op jit(solution)/shard_map/ppermute | solution.py:175
  2.2 14.4 %collective-permute-start.1 = (bf16[2,4096]{1,0:T(2,128)(2,1)}, bf16[2,4096]{1,0:T(2,128)(2,1)S(1)}, u32[]{:S(2)}, u32[]{:S(2)}) collective-permute-start(bf16[2,4096]{1,0:T(2,128)(2,1)} %param.3), channel_id=1, source_target_pairs={{16,0},{17,1},{18,2},{19,3},{20,4},{21,5},{22,6},{23,7},{24,8},{25... | collective-permute-start | bytes 49160 | tf_op jit(solution)/shard_map/ppermute | solution.py:175
  4.9 11.7 %collective-permute-start = (bf16[2,4096]{1,0:T(2,128)(2,1)}, bf16[2,4096]{1,0:T(2,128)(2,1)S(1)}, u32[]{:S(2)}, u32[]{:S(2)}) collective-permute-start(bf16[2,4096]{1,0:T(2,128)(2,1)} %param.3), channel_id=1, source_target_pairs={{8,0},{9,1},{10,2},{11,3},{12,4},{13,5},{14,6},{15,7},{16,8},{17,9... | collective-permute-start | bytes 49160 | tf_op jit(solution)/shard_map/ppermute | solution.py:175
  8.0 23.8 %all-to-all-start = ((bf16[8,8,4096]{2,1,0:T(8,128)(2,1)}), bf16[8,8,4096]{2,1,0:T(8,128)(2,1)S(1)}, u32[]{:S(2)}, u32[]{:S(2)}) async-start(bf16[8,8,4096]{2,1,0:T(8,128)(2,1)} %broadcast_in_dim.2), calls=%async_computation | async-start | bytes 1048576 | tf_op jit(solution)/shard_map/all_to_all | solution.py:190
  17.5 5.9 %collective-permute-start.5 = (bf16[8,4096]{1,0:T(8,128)(2,1)S(1)}, bf16[8,4096]{1,0:T(8,128)(2,1)S(1)}, u32[]{:S(2)}, u32[]{:S(2)}) collective-permute-start(bf16[8,4096]{1,0:T(8,128)(2,1)S(1)} %pad_maximum_fusion), channel_id=1, source_target_pairs={{6,0},{7,1},{0,2},{1,3},{2,4},{3,5},{4,6},{5,7},{14,8},{15,9},{8,1... | collective-permute-start | bytes 196616 | tf_op jit(solution)/shard_map/ppermute | solution.py:175
  19.1 5.8 %collective-permute-start.4 = (bf16[8,4096]{1,0:T(8,128)(2,1)S(1)}, bf16[8,4096]{1,0:T(8,128)(2,1)S(1)}, u32[]{:S(2)}, u32[]{:S(2)}) collective-permute-start(bf16[8,4096]{1,0:T(8,128)(2,1)S(1)} %pad_maximum_fusion), channel_id=1, source_target_pairs={{4,0},{5,1},{6,2},{7,3},{0,4},{1,5},{2,6},{3,7},{12,8},{13,9},{14,... | collective-permute-start | bytes 196616 | tf_op jit(solution)/shard_map/ppermute | solution.py:175
  22.0 4.3 %collective-permute-start.3 = (bf16[8,4096]{1,0:T(8,128)(2,1)S(1)}, bf16[8,4096]{1,0:T(8,128)(2,1)S(1)}, u32[]{:S(2)}, u32[]{:S(2)}) collective-permute-start(bf16[8,4096]{1,0:T(8,128)(2,1)S(1)} %pad_maximum_fusion), channel_id=1, source_target_pairs={{2,0},{3,1},{4,2},{5,3},{6,4},{7,5},{0,6},{1,7},{10,8},{11,9},{12,... | collective-permute-start | bytes 196616 | tf_op jit(solution)/shard_map/ppermute | solution.py:175
  27.1 1.8 collective-permute-start.6
  31.8 0.7 copy-start
  42.9 104.2 %collective-permute-start.7 = (f32[4096]{0:T(1024)S(1)}, f32[4096]{0:T(1024)S(1)}, u32[]{:S(2)}, u32[]{:S(2)}) collective-permute-start(f32[4096]{0:T(1024)S(1)} %bitcast.12), channel_id=1, source_target_pairs={{1,0},{0,1},{3,2},{2,3},{5,4},{4,5},{7,6},{6,7},{9,8},{8,9},{11,10... | collective-permute-start | bytes 49160 | tf_op jit(solution)/shard_map/ppermute | solution.py:175
  147.2 6.4 %collective-permute-start.10 = (f32[4096]{0:T(1024)S(1)}, f32[4096]{0:T(1024)S(1)}, u32[]{:S(2)}, u32[]{:S(2)}) collective-permute-start(f32[4096]{0:T(1024)S(1)} %multiply_add_fusion.2), channel_id=1, source_target_pairs={{16,0},{17,1},{18,2},{19,3},{20,4},{21,5},{22,6},{23,7},{24,8},{25... | collective-permute-start | bytes 49160 | tf_op jit(solution)/shard_map/ppermute | solution.py:175
  147.3 8.1 %collective-permute-start.9 = (f32[4096]{0:T(1024)S(1)}, f32[4096]{0:T(1024)S(1)}, u32[]{:S(2)}, u32[]{:S(2)}) collective-permute-start(f32[4096]{0:T(1024)S(1)} %multiply_add_fusion.2), channel_id=1, source_target_pairs={{24,0},{25,1},{26,2},{27,3},{28,4},{29,5},{30,6},{31,7},{0,8},{1,9... | collective-permute-start | bytes 49160 | tf_op jit(solution)/shard_map/ppermute | solution.py:175
  151.5 3.8 %collective-permute-start.8 = (f32[4096]{0:T(1024)S(1)}, f32[4096]{0:T(1024)S(1)}, u32[]{:S(2)}, u32[]{:S(2)}) collective-permute-start(f32[4096]{0:T(1024)S(1)} %multiply_add_fusion.2), channel_id=1, source_target_pairs={{8,0},{9,1},{10,2},{11,3},{12,4},{13,5},{14,6},{15,7},{16,8},{17,9... | collective-permute-start | bytes 49160 | tf_op jit(solution)/shard_map/ppermute | solution.py:175
  155.4 7.0 %collective-permute-start.13 = (f32[4096]{0:T(1024)S(1)}, f32[4096]{0:T(1024)S(1)}, u32[]{:S(2)}, u32[]{:S(2)}) collective-permute-start(f32[4096]{0:T(1024)S(1)} %multiply_add_fusion.1), channel_id=1, source_target_pairs={{4,0},{5,1},{6,2},{7,3},{0,4},{1,5},{2,6},{3,7},{12,8},{13,9},{14,... | collective-permute-start | bytes 49160 | tf_op jit(solution)/shard_map/ppermute | solution.py:175
  159.1 4.9 %collective-permute-start.12 = (f32[4096]{0:T(1024)S(1)}, f32[4096]{0:T(1024)S(1)}, u32[]{:S(2)}, u32[]{:S(2)}) collective-permute-start(f32[4096]{0:T(1024)S(1)} %multiply_add_fusion.1), channel_id=1, source_target_pairs={{6,0},{7,1},{0,2},{1,3},{2,4},{3,5},{4,6},{5,7},{14,8},{15,9},{8,1... | collective-permute-start | bytes 49160 | tf_op jit(solution)/shard_map/ppermute | solution.py:175
  159.8 4.2 %collective-permute-start.11 = (f32[4096]{0:T(1024)S(1)}, f32[4096]{0:T(1024)S(1)}, u32[]{:S(2)}, u32[]{:S(2)}) collective-permute-start(f32[4096]{0:T(1024)S(1)} %multiply_add_fusion.1), channel_id=1, source_target_pairs={{2,0},{3,1},{4,2},{5,3},{6,4},{7,5},{0,6},{1,7},{10,8},{11,9},{12,... | collective-permute-start | bytes 49160 | tf_op jit(solution)/shard_map/ppermute | solution.py:175

commit v3 on v2

--- a/solution.py
+++ b/solution.py
@@ -33,9 +33,8 @@
     rows = jnp.where(row == 0, hi.astype(jnp.float32), 0.0)
     rows = jnp.where(row == 1, mid.astype(jnp.float32), rows)
     rows = jnp.where(row == 2, low.astype(jnp.float32), rows)
-    points = points.astype(jnp.float32)
-    lhs[:, : 2 * d] = jnp.concatenate([points, rows], axis=0).T.astype(jnp.bfloat16)
-    lhs[:, 2 * d :] = jnp.concatenate([points, points], axis=0).T.astype(jnp.bfloat16)
+    lhs[:, : 2 * d] = jnp.concatenate([points, rows.astype(jnp.bfloat16)], axis=0).T
+    lhs[:, 2 * d :] = jnp.concatenate([points, points], axis=0).T
 
 
 def fill_fixed(points, rhs):
@@ -92,17 +91,15 @@
     return top + jnp.log2(jnp.exp2(parts - top).sum(0, keepdims=True))
 
 
-def joined(pieces):
-    return jnp.concatenate([piece[...].astype(jnp.float32) for piece in pieces], axis=0)
-
-
 def first_kernel(order, near, far, tgt, pot, *refs):
-    weights, (out, shift, flag, src, lhs, rhs) = refs[:KEPT], refs[KEPT:]
+    weights, (out, shift, flag, src, src_norm, tgt_norm, lhs, rhs) = refs[:KEPT], refs[KEPT:]
     share = weights[0].shape[0]
-    features = joined([near, far]).astype(jnp.bfloat16)
+    features = jnp.concatenate([near[...], far[...]], axis=0)
     src[...] = jnp.dot(order[...], features, preferred_element_type=jnp.float32).astype(jnp.bfloat16)
     fill_fixed(src[...], rhs)
-    bias = KAPPA * (pot[...] - square_norm(tgt[...]))
+    src_norm[...] = square_norm(src[...])
+    tgt_norm[...] = square_norm(tgt[...])
+    bias = pot[...] - KAPPA * tgt_norm[...]
     offset = jnp.max(bias, axis=1, keepdims=True) - HEAD
     shift[...] = bias - offset
     fill_streamed(tgt[...], bias - offset, lhs)
@@ -130,12 +127,13 @@
         exact_lse(lhs, rhs, out, offset)
 
 
-def second_kernel(tgt_total, src_total, lse, flag, shift, src, tgt, *refs):
-    weights, (new, base, out, factors, lhs, rhs) = refs[:KEPT], refs[KEPT:]
+def second_kernel(tgt_total, lse, flag, shift, src, tgt, src_norm, *refs):
+    weights, (new_out, out, factors, lhs, rhs, new, sem) = refs[:KEPT], refs[KEPT:]
     share, n_src = weights[0].shape
     bias = math.log2(tgt_total) - lse[...]
-    new[...] = square_norm(src[...]) + EPS * LN2 * bias
-    base[...] = square_norm(tgt[...]) + EPS * math.log(src_total)
+    new[...] = src_norm[...] + EPS * LN2 * bias
+    leave = pltpu.make_async_copy(new, new_out, sem)
+    leave.start()
     top = jnp.max(bias, axis=1, keepdims=True)
     factors[...] = jnp.broadcast_to(jnp.exp2(bias - top), (8, n_src))
 
@@ -157,6 +155,8 @@
         fill_fixed(tgt[...], rhs)
         exact_lse(lhs, rhs, out, 0.0)
 
+    leave.wait()
+
 
 ROW, X, Y, CORE = 8, 4, 4, 2
 
@@ -212,7 +212,7 @@
     order = feature_order(per_src, per_tgt)
 
     src = source_points
-    pot = target_potential.reshape(1, n_tgt)
+    pot = KAPPA * target_potential.reshape(1, n_tgt)
     copies = jnp.broadcast_to(target_points[None], (ROW,) + target_points.shape)
 
     tgt = all_to_all(copies, "row")
@@ -224,7 +224,7 @@
     f32, bf16 = jnp.float32, jnp.bfloat16
     whole, scalar = pl.BlockSpec(memory_space=pltpu.VMEM), pl.BlockSpec(memory_space=pltpu.SMEM)
     tgt = tgt.reshape(dim, n_tgt)
-    *weights, lse, shift, flag, src = pl.pallas_call(
+    *weights, lse, shift, flag, src, src_norm, tgt_norm = pl.pallas_call(
         first_kernel,
         out_shape=[
             *[pltpu.VMEM((n_tgt // KEPT, n_src), bf16)] * KEPT,
@@ -232,8 +232,10 @@
             jax.ShapeDtypeStruct((1, n_tgt), f32),
             jax.ShapeDtypeStruct((1, 1), jnp.int32),
             jax.ShapeDtypeStruct((dim, n_src), bf16),
+            jax.ShapeDtypeStruct((1, n_src), f32),
+            jax.ShapeDtypeStruct((1, n_tgt), f32),
         ],
-        out_specs=[whole] * KEPT + [whole, whole, scalar, whole],
+        out_specs=[whole] * KEPT + [whole, whole, scalar, whole, whole, whole],
         scratch_shapes=[
             pltpu.VMEM((n_tgt, 4 * dim), bf16),
             pltpu.VMEM((4 * dim, n_src), bf16),
@@ -247,25 +249,23 @@
     lse = ring_lse(lse, [from_col(lse, k, 0, 0) for k in (1, 2, 3)])
     lse = ring_lse(lse, [from_col(lse, 0, k, 0) for k in (1, 2, 3)])
 
-    source_new, base, parts = pl.pallas_call(
-        functools.partial(second_kernel, tgt_total, src_total),
-        out_shape=[
-            jax.ShapeDtypeStruct((1, n_src), f32),
-            jax.ShapeDtypeStruct((1, n_tgt), f32),
-            jax.ShapeDtypeStruct((ROW, n_tgt), f32),
-        ],
-        in_specs=[whole, scalar, whole, whole, whole] + [whole] * KEPT,
-        out_specs=[whole, whole, whole],
+    source_new, parts = pl.pallas_call(
+        functools.partial(second_kernel, tgt_total),
+        out_shape=[jax.ShapeDtypeStruct((1, n_src), f32), jax.ShapeDtypeStruct((ROW, n_tgt), f32)],
+        in_specs=[whole, scalar, whole, whole, whole, whole] + [whole] * KEPT,
+        out_specs=[pl.BlockSpec(memory_space=pl.ANY), whole],
         scratch_shapes=[
             pltpu.VMEM((8, n_src), f32),
             pltpu.VMEM((n_src, 4 * dim), bf16),
             pltpu.VMEM((4 * dim, n_tgt), bf16),
+            pltpu.VMEM((1, n_src), f32),
+            pltpu.SemaphoreType.DMA,
         ],
         compiler_params=params,
         name="second_pass",
-    )(lse.reshape(1, n_src), flag, shift, src, tgt, *weights)
+    )(lse.reshape(1, n_src), flag, shift, src, tgt, src_norm, *weights)
     parts = all_to_all(parts.reshape(ROW, 1, n_tgt), "row")
-    target_new = base.reshape(n_tgt) - EPS * LN2 * lse_of(parts).reshape(n_tgt)
+    target_new = tgt_norm.reshape(n_tgt) - EPS * LN2 * lse_of(parts).reshape(n_tgt) + EPS * math.log(src_total)
     return source_new.reshape(n_src), target_new
 
 

time: 294 us -> 293 us (level)
  no operation moved by 1% of the time
where the time goes in v3:
time: 293 us; the launch traced here: 291 us
  starting transfers between devices  137 us (47%)
  Pallas kernels  125 us (43%)
  blocking collectives  11.4 us (4%)
  waiting for transfers between devices  10.8 us (4%)
    ppermute x14, starting transfers between devices, from_col(): return lax.ppermute(v, 'col', pairs)  129 us
    pallas_call x1, Pallas kernels, on_device(): pl.pallas_call(functools.partial(second_kernel, tgt_total), out_shape=[ja...  115 us
    all_to_all x1, blocking collectives, all_to_all(): return lax.all_to_all(parts, axis, 0, 0, tiled=True)  11.4 us
    pallas_call x1, Pallas kernels, on_device(): pl.pallas_call(first_kernel, out_shape=[*[pltpu.VMEM((n_tgt // KEPT, n_sr...  10.5 us
    all_to_all x1, starting transfers between devices, all_to_all(): return lax.all_to_all(parts, axis, 0, 0, tiled=True)  8.57 us
    ppermute x14, waiting for transfers between devices, from_col(): return lax.ppermute(v, 'col', pairs)  7.94 us
  transfers between devices with their start and end apart: 15, of which 7 were waited for; matrix products, arithmetic and copies ran while one was open for 1% of the time, Pallas kernels for 0%

profile of v3, /device:TPU:32, one launch (start us, length us, event | category | flops | bytes accessed | tf_op | source)
XLA Modules:
  0.0 290.5 jit_solution(9086212085466602371)
XLA Ops:
  0.6 1.6 collective-permute-start.2
  2.2 2.7 collective-permute-start.1
  4.9 1.4 collective-permute-start
  6.4 1.7 broadcast_in_dim.2
  8.0 8.6 %all-to-all-start = ((bf16[8,8,4096]{2,1,0:T(8,128)(2,1)}), bf16[8,8,4096]{2,1,0:T(8,128)(2,1)S(1)}, u32[]{:S(2)}, u32[]{:S(2)}) async-start(bf16[8,8,4096]{2,1,0:T(8,128)(2,1)} %broadcast_in_dim.2), calls=%async_computation | async-start | bytes 1048576 | tf_op jit(solution)/shard_map/all_to_all | solution.py:190
  16.7 0.8 pad_maximum_fusion
  17.5 1.7 collective-permute-start.5
  19.2 2.9 collective-permute-start.4
  22.1 1.3 collective-permute-start.3
  23.4 1.6 collective-permute-done.4
  25.0 1.3 collective-permute-done.3
  26.4 0.8 concatenate.8.near
  27.2 0.3 collective-permute-start.6
  27.5 0.7 broadcast_multiply_fusion
  28.2 0.8 collective-permute-done.6.far
  29.0 2.8 all-to-all-done
  31.8 10.5 %first_pass.1 = (bf16[512,4096]{1,0:T(8,128)(2,1)S(1)}, bf16[512,4096]{1,0:T(8,128)(2,1)S(1)}, bf16[512,4096]{1,0:T(8,128)(2,1)S(1)}, bf16[512,4096]{1,0:T(8,128...) custom-call(bf16[64,64]{1,0:T(8,128)(2,1)S(1)} %fusion.17.order, ...), custom_call_target="tpu_custom_call" | custom-call | tf_op jit(solution)/shard_map/first_pass/pallas_call | solution.py:227
  42.4 103.4 %collective-permute-start.7 = (f32[4096]{0:T(1024)S(1)}, f32[4096]{0:T(1024)S(1)}, u32[]{:S(2)}, u32[]{:S(2)}) collective-permute-start(f32[4096]{0:T(1024)S(1)} %bitcast.12), channel_id=1, source_target_pairs={{1,0},{0,1},{3,2},{2,3},{5,4},{4,5},{7,6},{6,7},{9,8},{8,9},{11,10... | collective-permute-start | bytes 49160 | tf_op jit(solution)/shard_map/ppermute | solution.py:175
  145.8 0.8 collective-permute-done.7
  146.7 3.6 %collective-permute-start.10 = (f32[4096]{0:T(1024)S(1)}, f32[4096]{0:T(1024)S(1)}, u32[]{:S(2)}, u32[]{:S(2)}) collective-permute-start(f32[4096]{0:T(1024)S(1)} %multiply_add_fusion.2), channel_id=1, source_target_pairs={{16,0},{17,1},{18,2},{19,3},{20,4},{21,5},{22,6},{23,7},{24,8},{25... | collective-permute-start | bytes 49160 | tf_op jit(solution)/shard_map/ppermute | solution.py:175
  150.3 0.4 collective-permute-start.9
  150.7 2.8 collective-permute-start.8
  153.5 1.7 collective-permute-done.9
  155.3 3.3 %collective-permute-start.13 = (f32[4096]{0:T(1024)S(1)}, f32[4096]{0:T(1024)S(1)}, u32[]{:S(2)}, u32[]{:S(2)}) collective-permute-start(f32[4096]{0:T(1024)S(1)} %multiply_add_fusion.1), channel_id=1, source_target_pairs={{4,0},{5,1},{6,2},{7,3},{0,4},{1,5},{2,6},{3,7},{12,8},{13,9},{14,... | collective-permute-start | bytes 49160 | tf_op jit(solution)/shard_map/ppermute | solution.py:175
  158.5 0.7 collective-permute-start.12
  159.2 2.5 collective-permute-start.11
  161.8 1.7 collective-permute-done.12
  163.5 114.5 %second_pass.1 = (f32[1,4096]{1,0:T(1,128)}, f32[8,4096]{1,0:T(8,128)S(1)}) custom-call(f32[1,4096]{1,0:T(1,128)S(1)} %bitcast.10, s32[1,1]{1,0:T(1,128)} %get-tuple-element.19.flag, f32[1,4096]{1,0:T(1,128)S(1)} %get-tuple-element.20.shift, bf16[64,4096]{1,0:T(8,128)(2,1)S(1)} %get-tuple-element.21.src, bf16[64,4096]{1,0:T(8,128)(2,1)S(1)} %bitcast.8, ...), custom_call_target="tpu_custom_call" | custom-call | tf_op jit(solution)/shard_map/second_pass/pallas_call | solution.py:252
  278.1 0.1 copy.6
  278.2 11.4 %all_to_all.10 = f32[8,1,4096]{2,1,0:T(1,128)S(1)} all-to-all(f32[8,1,4096]{2,1,0:T(1,128)S(1)} %copy.6), channel_id=1, replica_groups=mesh['row'=8,'col'=32] {'row'}, dimensions={0} | all-to-all | bytes 262144 | tf_op jit(solution)/shard_map/all_to_all | solution.py:190
  289.8 0.1 fusion.2
  289.9 0.6 subtract_add_fusion
  (19 shorter events, 0.3 us)
Async XLA Ops:
  0.6 16.1 %collective-permute-start.2 = (bf16[2,4096]{1,0:T(2,128)(2,1)}, bf16[2,4096]{1,0:T(2,128)(2,1)S(1)}, u32[]{:S(2)}, u32[]{:S(2)}) collective-permute-start(bf16[2,4096]{1,0:T(2,128)(2,1)} %param.3), channel_id=1, source_target_pairs={{24,0},{25,1},{26,2},{27,3},{28,4},{29,5},{30,6},{31,7},{0,8},{1,9... | collective-permute-start | bytes 49160 | tf_op jit(solution)/shard_map/ppermute | solution.py:175
  2.2 14.5 %collective-permute-start.1 = (bf16[2,4096]{1,0:T(2,128)(2,1)}, bf16[2,4096]{1,0:T(2,128)(2,1)S(1)}, u32[]{:S(2)}, u32[]{:S(2)}) collective-permute-start(bf16[2,4096]{1,0:T(2,128)(2,1)} %param.3), channel_id=1, source_target_pairs={{16,0},{17,1},{18,2},{19,3},{20,4},{21,5},{22,6},{23,7},{24,8},{25... | collective-permute-start | bytes 49160 | tf_op jit(solution)/shard_map/ppermute | solution.py:175
  4.9 11.8 %collective-permute-start = (bf16[2,4096]{1,0:T(2,128)(2,1)}, bf16[2,4096]{1,0:T(2,128)(2,1)S(1)}, u32[]{:S(2)}, u32[]{:S(2)}) collective-permute-start(bf16[2,4096]{1,0:T(2,128)(2,1)} %param.3), channel_id=1, source_target_pairs={{8,0},{9,1},{10,2},{11,3},{12,4},{13,5},{14,6},{15,7},{16,8},{17,9... | collective-permute-start | bytes 49160 | tf_op jit(solution)/shard_map/ppermute | solution.py:175
  8.0 23.8 %all-to-all-start = ((bf16[8,8,4096]{2,1,0:T(8,128)(2,1)}), bf16[8,8,4096]{2,1,0:T(8,128)(2,1)S(1)}, u32[]{:S(2)}, u32[]{:S(2)}) async-start(bf16[8,8,4096]{2,1,0:T(8,128)(2,1)} %broadcast_in_dim.2), calls=%async_computation | async-start | bytes 1048576 | tf_op jit(solution)/shard_map/all_to_all | solution.py:190
  17.5 5.9 %collective-permute-start.5 = (bf16[8,4096]{1,0:T(8,128)(2,1)S(1)}, bf16[8,4096]{1,0:T(8,128)(2,1)S(1)}, u32[]{:S(2)}, u32[]{:S(2)}) collective-permute-start(bf16[8,4096]{1,0:T(8,128)(2,1)S(1)} %pad_maximum_fusion), channel_id=1, source_target_pairs={{6,0},{7,1},{0,2},{1,3},{2,4},{3,5},{4,6},{5,7},{14,8},{15,9},{8,1... | collective-permute-start | bytes 196616 | tf_op jit(solution)/shard_map/ppermute | solution.py:175
  19.2 5.8 %collective-permute-start.4 = (bf16[8,4096]{1,0:T(8,128)(2,1)S(1)}, bf16[8,4096]{1,0:T(8,128)(2,1)S(1)}, u32[]{:S(2)}, u32[]{:S(2)}) collective-permute-start(bf16[8,4096]{1,0:T(8,128)(2,1)S(1)} %pad_maximum_fusion), channel_id=1, source_target_pairs={{4,0},{5,1},{6,2},{7,3},{0,4},{1,5},{2,6},{3,7},{12,8},{13,9},{14,... | collective-permute-start | bytes 196616 | tf_op jit(solution)/shard_map/ppermute | solution.py:175
  22.1 4.3 %collective-permute-start.3 = (bf16[8,4096]{1,0:T(8,128)(2,1)S(1)}, bf16[8,4096]{1,0:T(8,128)(2,1)S(1)}, u32[]{:S(2)}, u32[]{:S(2)}) collective-permute-start(bf16[8,4096]{1,0:T(8,128)(2,1)S(1)} %pad_maximum_fusion), channel_id=1, source_target_pairs={{2,0},{3,1},{4,2},{5,3},{6,4},{7,5},{0,6},{1,7},{10,8},{11,9},{12,... | collective-permute-start | bytes 196616 | tf_op jit(solution)/shard_map/ppermute | solution.py:175
  27.2 1.8 collective-permute-start.6
  42.4 104.3 %collective-permute-start.7 = (f32[4096]{0:T(1024)S(1)}, f32[4096]{0:T(1024)S(1)}, u32[]{:S(2)}, u32[]{:S(2)}) collective-permute-start(f32[4096]{0:T(1024)S(1)} %bitcast.12), channel_id=1, source_target_pairs={{1,0},{0,1},{3,2},{2,3},{5,4},{4,5},{7,6},{6,7},{9,8},{8,9},{11,10... | collective-permute-start | bytes 49160 | tf_op jit(solution)/shard_map/ppermute | solution.py:175
  146.7 6.9 %collective-permute-start.10 = (f32[4096]{0:T(1024)S(1)}, f32[4096]{0:T(1024)S(1)}, u32[]{:S(2)}, u32[]{:S(2)}) collective-permute-start(f32[4096]{0:T(1024)S(1)} %multiply_add_fusion.2), channel_id=1, source_target_pairs={{16,0},{17,1},{18,2},{19,3},{20,4},{21,5},{22,6},{23,7},{24,8},{25... | collective-permute-start | bytes 49160 | tf_op jit(solution)/shard_map/ppermute | solution.py:175
  150.3 5.0 %collective-permute-start.9 = (f32[4096]{0:T(1024)S(1)}, f32[4096]{0:T(1024)S(1)}, u32[]{:S(2)}, u32[]{:S(2)}) collective-permute-start(f32[4096]{0:T(1024)S(1)} %multiply_add_fusion.2), channel_id=1, source_target_pairs={{24,0},{25,1},{26,2},{27,3},{28,4},{29,5},{30,6},{31,7},{0,8},{1,9... | collective-permute-start | bytes 49160 | tf_op jit(solution)/shard_map/ppermute | solution.py:175
  150.7 4.6 %collective-permute-start.8 = (f32[4096]{0:T(1024)S(1)}, f32[4096]{0:T(1024)S(1)}, u32[]{:S(2)}, u32[]{:S(2)}) collective-permute-start(f32[4096]{0:T(1024)S(1)} %multiply_add_fusion.2), channel_id=1, source_target_pairs={{8,0},{9,1},{10,2},{11,3},{12,4},{13,5},{14,6},{15,7},{16,8},{17,9... | collective-permute-start | bytes 49160 | tf_op jit(solution)/shard_map/ppermute | solution.py:175
  155.3 6.5 %collective-permute-start.13 = (f32[4096]{0:T(1024)S(1)}, f32[4096]{0:T(1024)S(1)}, u32[]{:S(2)}, u32[]{:S(2)}) collective-permute-start(f32[4096]{0:T(1024)S(1)} %multiply_add_fusion.1), channel_id=1, source_target_pairs={{4,0},{5,1},{6,2},{7,3},{0,4},{1,5},{2,6},{3,7},{12,8},{13,9},{14,... | collective-permute-start | bytes 49160 | tf_op jit(solution)/shard_map/ppermute | solution.py:175
  158.5 4.9 %collective-permute-start.12 = (f32[4096]{0:T(1024)S(1)}, f32[4096]{0:T(1024)S(1)}, u32[]{:S(2)}, u32[]{:S(2)}) collective-permute-start(f32[4096]{0:T(1024)S(1)} %multiply_add_fusion.1), channel_id=1, source_target_pairs={{6,0},{7,1},{0,2},{1,3},{2,4},{3,5},{4,6},{5,7},{14,8},{15,9},{8,1... | collective-permute-start | bytes 49160 | tf_op jit(solution)/shard_map/ppermute | solution.py:175
  159.2 4.3 %collective-permute-start.11 = (f32[4096]{0:T(1024)S(1)}, f32[4096]{0:T(1024)S(1)}, u32[]{:S(2)}, u32[]{:S(2)}) collective-permute-start(f32[4096]{0:T(1024)S(1)} %multiply_add_fusion.1), channel_id=1, source_target_pairs={{2,0},{3,1},{4,2},{5,3},{6,4},{7,5},{0,6},{1,7},{10,8},{11,9},{12,... | collective-permute-start | bytes 49160 | tf_op jit(solution)/shard_map/ppermute | solution.py:175

commit v4 on v3

--- a/solution.py
+++ b/solution.py
@@ -84,11 +84,6 @@
 
 def square_norm(points):
     return jnp.sum(jnp.square(points.astype(jnp.float32)), axis=0, keepdims=True)
-
-
-def lse_of(parts):
-    top = parts.max(0, keepdims=True)
-    return top + jnp.log2(jnp.exp2(parts - top).sum(0, keepdims=True))
 
 
 def first_kernel(order, near, far, tgt, pot, *refs):
@@ -173,6 +168,12 @@
                 there = (((x + kx) % X) * Y + (y + ky) % Y) * CORE + (c + kc) % CORE
                 pairs.append((there, (x * Y + y) * CORE + c))
     return lax.ppermute(v, "col", pairs)
+
+
+def lse_of_rows(parts):
+    rows = [parts[k] for k in range(ROW)]
+    top = functools.reduce(jnp.maximum, rows)
+    return top + jnp.log2(functools.reduce(jnp.add, [jnp.exp2(row - top) for row in rows]))
 
 
 def pair_lse(a, b):
@@ -265,7 +266,7 @@
         name="second_pass",
     )(lse.reshape(1, n_src), flag, shift, src, tgt, src_norm, *weights)
     parts = all_to_all(parts.reshape(ROW, 1, n_tgt), "row")
-    target_new = tgt_norm.reshape(n_tgt) - EPS * LN2 * lse_of(parts).reshape(n_tgt) + EPS * math.log(src_total)
+    target_new = tgt_norm.reshape(n_tgt) - EPS * LN2 * lse_of_rows(parts.reshape(ROW, n_tgt)) + EPS * math.log(src_total)
     return source_new.reshape(n_src), target_new
 
 

time: 293 us -> 293 us (level)
  no operation moved by 1% of the time
where the time goes in v4:
time: 293 us; the launch traced here: 290 us
  starting transfers between devices  137 us (47%)
  Pallas kernels  125 us (43%)
  blocking collectives  11.5 us (4%)
  waiting for transfers between devices  10.8 us (4%)
    ppermute x14, starting transfers between devices, from_col(): return lax.ppermute(v, 'col', pairs)  128 us
    pallas_call x1, Pallas kernels, on_device(): pl.pallas_call(functools.partial(second_kernel, tgt_total), out_shape=[ja...  115 us
    all_to_all x1, blocking collectives, all_to_all(): return lax.all_to_all(parts, axis, 0, 0, tiled=True)  11.5 us
    pallas_call x1, Pallas kernels, on_device(): pl.pallas_call(first_kernel, out_shape=[*[pltpu.VMEM((n_tgt // KEPT, n_sr...  10.5 us
    all_to_all x1, starting transfers between devices, all_to_all(): return lax.all_to_all(parts, axis, 0, 0, tiled=True)  8.57 us
    ppermute x14, waiting for transfers between devices, from_col(): return lax.ppermute(v, 'col', pairs)  7.94 us
  transfers between devices with their start and end apart: 15, of which 7 were waited for; matrix products, arithmetic and copies ran while one was open for 1% of the time, Pallas kernels for 0%

profile of v4, /device:TPU:32, one launch (start us, length us, event | category | flops | bytes accessed | tf_op | source)
XLA Modules:
  0.0 289.9 jit_solution(12207016496372733263)
XLA Ops:
  0.6 1.6 collective-permute-start.2
  2.2 2.7 collective-permute-start.1
  4.9 1.4 collective-permute-start
  6.4 1.7 broadcast_in_dim.2
  8.0 8.6 %all-to-all-start = ((bf16[8,8,4096]{2,1,0:T(8,128)(2,1)}), bf16[8,8,4096]{2,1,0:T(8,128)(2,1)S(1)}, u32[]{:S(2)}, u32[]{:S(2)}) async-start(bf16[8,8,4096]{2,1,0:T(8,128)(2,1)} %broadcast_in_dim.2), calls=%async_computation | async-start | bytes 1048576 | tf_op jit(solution)/shard_map/all_to_all | solution.py:191
  16.7 0.0 collective-permute-done.1
  16.7 0.8 pad_maximum_fusion
  17.5 1.7 collective-permute-start.5
  19.2 2.9 %collective-permute-start.4 = (bf16[8,4096]{1,0:T(8,128)(2,1)S(1)}, bf16[8,4096]{1,0:T(8,128)(2,1)S(1)}, u32[]{:S(2)}, u32[]{:S(2)}) collective-permute-start(bf16[8,4096]{1,0:T(8,128)(2,1)S(1)} %pad_maximum_fusion), channel_id=1, source_target_pairs={{4,0},{5,1},{6,2},{7,3},{0,4},{1,5},{2,6},{3,7},{12,8},{13,9},{14,... | collective-permute-start | bytes 196616 | tf_op jit(solution)/shard_map/ppermute | solution.py:170
  22.1 1.3 collective-permute-start.3
  23.4 1.6 collective-permute-done.4
  25.0 1.3 collective-permute-done.3
  26.4 0.8 concatenate.8.near
  27.2 0.3 collective-permute-start.6
  27.5 0.7 broadcast_multiply_fusion
  28.2 0.8 collective-permute-done.6.far
  29.0 2.8 all-to-all-done
  31.8 10.5 %first_pass.1 = (bf16[512,4096]{1,0:T(8,128)(2,1)S(1)}, bf16[512,4096]{1,0:T(8,128)(2,1)S(1)}, bf16[512,4096]{1,0:T(8,128)(2,1)S(1)}, bf16[512,4096]{1,0:T(8,128...) custom-call(bf16[64,64]{1,0:T(8,128)(2,1)S(1)} %fusion.14.order, ...), custom_call_target="tpu_custom_call" | custom-call | tf_op jit(solution)/shard_map/first_pass/pallas_call | solution.py:228
  42.3 103.4 %collective-permute-start.7 = (f32[4096]{0:T(1024)S(1)}, f32[4096]{0:T(1024)S(1)}, u32[]{:S(2)}, u32[]{:S(2)}) collective-permute-start(f32[4096]{0:T(1024)S(1)} %bitcast.21), channel_id=1, source_target_pairs={{1,0},{0,1},{3,2},{2,3},{5,4},{4,5},{7,6},{6,7},{9,8},{8,9},{11,10... | collective-permute-start | bytes 49160 | tf_op jit(solution)/shard_map/ppermute | solution.py:170
  145.8 0.8 collective-permute-done.7
  146.7 3.6 %collective-permute-start.10 = (f32[4096]{0:T(1024)S(1)}, f32[4096]{0:T(1024)S(1)}, u32[]{:S(2)}, u32[]{:S(2)}) collective-permute-start(f32[4096]{0:T(1024)S(1)} %multiply_add_fusion.2), channel_id=1, source_target_pairs={{16,0},{17,1},{18,2},{19,3},{20,4},{21,5},{22,6},{23,7},{24,8},{25... | collective-permute-start | bytes 49160 | tf_op jit(solution)/shard_map/ppermute | solution.py:170
  150.3 0.4 collective-permute-start.9
  150.7 2.8 collective-permute-start.8
  153.5 1.7 collective-permute-done.9
  155.3 2.8 collective-permute-start.13
  158.1 1.2 collective-permute-start.12
  159.2 2.1 collective-permute-start.11
  161.3 1.7 collective-permute-done.12
  163.1 114.5 %second_pass.1 = (f32[1,4096]{1,0:T(1,128)}, f32[8,4096]{1,0:T(8,128)S(1)}) custom-call(f32[1,4096]{1,0:T(1,128)S(1)} %bitcast.18, s32[1,1]{1,0:T(1,128)} %get-tuple-element.19.flag, f32[1,4096]{1,0:T(1,128)S(1)} %get-tuple-element.20.shift, bf16[64,4096]{1,0:T(8,128)(2,1)S(1)} %get-tuple-element.21.src, bf16[64,4096]{1,0:T(8,128)(2,1)S(1)} %bitcast.16, ...), custom_call_target="tpu_custom_call" | custom-call | tf_op jit(solution)/shard_map/second_pass/pallas_call | solution.py:253
  277.6 0.1 copy.5
  277.8 11.5 %all_to_all.10 = f32[8,1,4096]{2,1,0:T(1,128)S(1)} all-to-all(f32[8,1,4096]{2,1,0:T(1,128)S(1)} %copy.5), channel_id=1, replica_groups=mesh['row'=8,'col'=32] {'row'}, dimensions={0} | all-to-all | bytes 262144 | tf_op jit(solution)/shard_map/all_to_all | solution.py:191
  289.3 0.7 subtract_add_fusion
  (18 shorter events, 0.2 us)
Async XLA Ops:
  0.6 16.1 %collective-permute-start.2 = (bf16[2,4096]{1,0:T(2,128)(2,1)}, bf16[2,4096]{1,0:T(2,128)(2,1)S(1)}, u32[]{:S(2)}, u32[]{:S(2)}) collective-permute-start(bf16[2,4096]{1,0:T(2,128)(2,1)} %param.3), channel_id=1, source_target_pairs={{24,0},{25,1},{26,2},{27,3},{28,4},{29,5},{30,6},{31,7},{0,8},{1,9... | collective-permute-start | bytes 49160 | tf_op jit(solution)/shard_map/ppermute | solution.py:170
  2.2 14.5 %collective-permute-start.1 = (bf16[2,4096]{1,0:T(2,128)(2,1)}, bf16[2,4096]{1,0:T(2,128)(2,1)S(1)}, u32[]{:S(2)}, u32[]{:S(2)}) collective-permute-start(bf16[2,4096]{1,0:T(2,128)(2,1)} %param.3), channel_id=1, source_target_pairs={{16,0},{17,1},{18,2},{19,3},{20,4},{21,5},{22,6},{23,7},{24,8},{25... | collective-permute-start | bytes 49160 | tf_op jit(solution)/shard_map/ppermute | solution.py:170
  4.9 11.8 %collective-permute-start = (bf16[2,4096]{1,0:T(2,128)(2,1)}, bf16[2,4096]{1,0:T(2,128)(2,1)S(1)}, u32[]{:S(2)}, u32[]{:S(2)}) collective-permute-start(bf16[2,4096]{1,0:T(2,128)(2,1)} %param.3), channel_id=1, source_target_pairs={{8,0},{9,1},{10,2},{11,3},{12,4},{13,5},{14,6},{15,7},{16,8},{17,9... | collective-permute-start | bytes 49160 | tf_op jit(solution)/shard_map/ppermute | solution.py:170
  8.0 23.8 %all-to-all-start = ((bf16[8,8,4096]{2,1,0:T(8,128)(2,1)}), bf16[8,8,4096]{2,1,0:T(8,128)(2,1)S(1)}, u32[]{:S(2)}, u32[]{:S(2)}) async-start(bf16[8,8,4096]{2,1,0:T(8,128)(2,1)} %broadcast_in_dim.2), calls=%async_computation | async-start | bytes 1048576 | tf_op jit(solution)/shard_map/all_to_all | solution.py:191
  17.5 5.9 %collective-permute-start.5 = (bf16[8,4096]{1,0:T(8,128)(2,1)S(1)}, bf16[8,4096]{1,0:T(8,128)(2,1)S(1)}, u32[]{:S(2)}, u32[]{:S(2)}) collective-permute-start(bf16[8,4096]{1,0:T(8,128)(2,1)S(1)} %pad_maximum_fusion), channel_id=1, source_target_pairs={{6,0},{7,1},{0,2},{1,3},{2,4},{3,5},{4,6},{5,7},{14,8},{15,9},{8,1... | collective-permute-start | bytes 196616 | tf_op jit(solution)/shard_map/ppermute | solution.py:170
  19.2 5.8 %collective-permute-start.4 = (bf16[8,4096]{1,0:T(8,128)(2,1)S(1)}, bf16[8,4096]{1,0:T(8,128)(2,1)S(1)}, u32[]{:S(2)}, u32[]{:S(2)}) collective-permute-start(bf16[8,4096]{1,0:T(8,128)(2,1)S(1)} %pad_maximum_fusion), channel_id=1, source_target_pairs={{4,0},{5,1},{6,2},{7,3},{0,4},{1,5},{2,6},{3,7},{12,8},{13,9},{14,... | collective-permute-start | bytes 196616 | tf_op jit(solution)/shard_map/ppermute | solution.py:170
  22.1 4.3 %collective-permute-start.3 = (bf16[8,4096]{1,0:T(8,128)(2,1)S(1)}, bf16[8,4096]{1,0:T(8,128)(2,1)S(1)}, u32[]{:S(2)}, u32[]{:S(2)}) collective-permute-start(bf16[8,4096]{1,0:T(8,128)(2,1)S(1)} %pad_maximum_fusion), channel_id=1, source_target_pairs={{2,0},{3,1},{4,2},{5,3},{6,4},{7,5},{0,6},{1,7},{10,8},{11,9},{12,... | collective-permute-start | bytes 196616 | tf_op jit(solution)/shard_map/ppermute | solution.py:170
  27.2 1.8 collective-permute-start.6
  42.3 104.3 %collective-permute-start.7 = (f32[4096]{0:T(1024)S(1)}, f32[4096]{0:T(1024)S(1)}, u32[]{:S(2)}, u32[]{:S(2)}) collective-permute-start(f32[4096]{0:T(1024)S(1)} %bitcast.21), channel_id=1, source_target_pairs={{1,0},{0,1},{3,2},{2,3},{5,4},{4,5},{7,6},{6,7},{9,8},{8,9},{11,10... | collective-permute-start | bytes 49160 | tf_op jit(solution)/shard_map/ppermute | solution.py:170
  146.7 6.9 %collective-permute-start.10 = (f32[4096]{0:T(1024)S(1)}, f32[4096]{0:T(1024)S(1)}, u32[]{:S(2)}, u32[]{:S(2)}) collective-permute-start(f32[4096]{0:T(1024)S(1)} %multiply_add_fusion.2), channel_id=1, source_target_pairs={{16,0},{17,1},{18,2},{19,3},{20,4},{21,5},{22,6},{23,7},{24,8},{25... | collective-permute-start | bytes 49160 | tf_op jit(solution)/shard_map/ppermute | solution.py:170
  150.3 5.0 %collective-permute-start.9 = (f32[4096]{0:T(1024)S(1)}, f32[4096]{0:T(1024)S(1)}, u32[]{:S(2)}, u32[]{:S(2)}) collective-permute-start(f32[4096]{0:T(1024)S(1)} %multiply_add_fusion.2), channel_id=1, source_target_pairs={{24,0},{25,1},{26,2},{27,3},{28,4},{29,5},{30,6},{31,7},{0,8},{1,9... | collective-permute-start | bytes 49160 | tf_op jit(solution)/shard_map/ppermute | solution.py:170
  150.7 4.6 %collective-permute-start.8 = (f32[4096]{0:T(1024)S(1)}, f32[4096]{0:T(1024)S(1)}, u32[]{:S(2)}, u32[]{:S(2)}) collective-permute-start(f32[4096]{0:T(1024)S(1)} %multiply_add_fusion.2), channel_id=1, source_target_pairs={{8,0},{9,1},{10,2},{11,3},{12,4},{13,5},{14,6},{15,7},{16,8},{17,9... | collective-permute-start | bytes 49160 | tf_op jit(solution)/shard_map/ppermute | solution.py:170
  155.3 6.0 %collective-permute-start.13 = (f32[4096]{0:T(1024)S(1)}, f32[4096]{0:T(1024)S(1)}, u32[]{:S(2)}, u32[]{:S(2)}) collective-permute-start(f32[4096]{0:T(1024)S(1)} %multiply_add_fusion.1), channel_id=1, source_target_pairs={{4,0},{5,1},{6,2},{7,3},{0,4},{1,5},{2,6},{3,7},{12,8},{13,9},{14,... | collective-permute-start | bytes 49160 | tf_op jit(solution)/shard_map/ppermute | solution.py:170
  158.1 4.9 %collective-permute-start.12 = (f32[4096]{0:T(1024)S(1)}, f32[4096]{0:T(1024)S(1)}, u32[]{:S(2)}, u32[]{:S(2)}) collective-permute-start(f32[4096]{0:T(1024)S(1)} %multiply_add_fusion.1), channel_id=1, source_target_pairs={{6,0},{7,1},{0,2},{1,3},{2,4},{3,5},{4,6},{5,7},{14,8},{15,9},{8,1... | collective-permute-start | bytes 49160 | tf_op jit(solution)/shard_map/ppermute | solution.py:170
  159.2 3.8 %collective-permute-start.11 = (f32[4096]{0:T(1024)S(1)}, f32[4096]{0:T(1024)S(1)}, u32[]{:S(2)}, u32[]{:S(2)}) collective-permute-start(f32[4096]{0:T(1024)S(1)} %multiply_add_fusion.1), channel_id=1, source_target_pairs={{2,0},{3,1},{4,2},{5,3},{6,4},{7,5},{0,6},{1,7},{10,8},{11,9},{12,... | collective-permute-start | bytes 49160 | tf_op jit(solution)/shard_map/ppermute | solution.py:170
